TPU v7x, 128 devices: a whole 4x4x4 slice. The times are simulated.
128 devices in a mesh: nodes: 128 (over x, y, z, core).
Axes of the slice: x: 4, y: 4, z: 4, core: 2. Of those that a mesh axis runs over, the one named last changes fastest.
Arguments:
- features: bfloat16 [262144, 128], P('nodes'), may hold values from -6 to 6
- weight: bfloat16 [128, 256], replicated, may hold values from -0.5 to 0.5
- cotangent: bfloat16 [262144, 256], P('nodes'), may hold values from -6 to 6
- block_pairs: int32 [12288, 2], P('nodes'), may hold values from 0 to 1023, as said below
- tile_counts: int32 [128], P('nodes'), may hold values from 48 to 96, as said below
- tile_values: bfloat16 [12288, 256, 256], P('nodes'), may hold values from -0.125 to 0.125
Outputs:
- hidden: bfloat16 [262144, 256], P('nodes')
- weight_grad: float32 [128, 256], replicated
- feature_grad: bfloat16 [262144, 128], P('nodes')
Inputs may be any that keep to these rules, and one draw needn't show every extreme that they name: `block_pairs`: every live slot of device d has its row block homed on d. Live slots of one device name at most one column block homed on any other device, and some device names blocks of min(72, 128 - 1) other devices. Slots after the live ones hold the pair (d * 8, d * 8). `tile_counts`: some device in every draw has all 96 slots live.
All inputs are finite; a program needn't handle non-finite values.
Results may differ from a plain program's by a relative error of at most 0.0075.
Values may be sent and summed in bfloat16 or wider, within the bound.
No kernel may reach another device: no remote copies, remote signals or barrier semaphores. Data moves between devices by JAX's collectives and lax.ppermute only.
A program may use at most 192 MiB of HBM per device.

v0:
```python
import jax
import jax.numpy as jnp
from jax import lax
from jax.sharding import PartitionSpec as P


def aggregate(
    blocks, tile_values, row_local, col_blocks, home, remote, live, asked, slot_of, peers_total
):
    local_blocks = blocks.shape[0]
    own_rows = jnp.take(blocks, row_local, axis=0)
    transposed = jnp.einsum(
        "jab,jaf->jbf", tile_values, own_rows, preferred_element_type=jnp.float32
    )
    rounded = transposed.astype(jnp.bfloat16)
    outgoing = jnp.where(
        (slot_of >= 0)[:, None, None],
        jnp.take(rounded, jnp.maximum(slot_of, 0), axis=0),
        jnp.zeros((), jnp.bfloat16),
    )
    sending = jnp.where(
        (asked >= 0)[:, None, None],
        jnp.take(blocks, jnp.maximum(asked, 0), axis=0),
        jnp.zeros((), jnp.bfloat16),
    )
    arrived = lax.all_to_all(sending, "nodes", split_axis=0, concat_axis=0, tiled=True)
    table = jnp.concatenate([arrived, blocks], 0)
    pick = jnp.where(remote, home, peers_total + col_blocks % local_blocks)
    fetched = jnp.take(table, pick, axis=0)
    direct = jnp.einsum("jab,jbf->jaf", tile_values, fetched, preferred_element_type=jnp.float32)
    returned = lax.all_to_all(outgoing, "nodes", split_axis=0, concat_axis=0, tiled=True)
    block_ids = jnp.arange(local_blocks, dtype=jnp.int32)
    row_hot = (live[:, None] & (row_local[:, None] == block_ids[None, :])).astype(jnp.float32)
    col_hot = (
        (live & ~remote)[:, None] & ((col_blocks % local_blocks)[:, None] == block_ids[None, :])
    ).astype(jnp.float32)
    totals = jnp.einsum("jk,jaf->kaf", row_hot, direct, precision=lax.Precision.HIGHEST)
    totals = totals + jnp.einsum(
        "jk,jaf->kaf", col_hot, transposed, precision=lax.Precision.HIGHEST
    )
    asked_hot = (asked[:, None] == block_ids[None, :]).astype(jnp.bfloat16)
    totals = totals + jnp.einsum(
        "qk,qaf->kaf", asked_hot, returned, preferred_element_type=jnp.float32
    )
    return totals


def on_device(features, weight, cotangent, block_pairs, tile_counts, tile_values):
    peers_total = lax.axis_size("nodes")
    myself = lax.axis_index("nodes")
    block_rows = tile_values.shape[1]
    width_in = features.shape[1]
    local_blocks = features.shape[0] // block_rows
    slot_total = block_pairs.shape[0]
    slot_ids = jnp.arange(slot_total, dtype=jnp.int32)
    peer_ids = jnp.arange(peers_total, dtype=jnp.int32)
    row_local = block_pairs[:, 0] - myself * local_blocks
    col_blocks = block_pairs[:, 1]
    home = col_blocks // local_blocks
    remote = home != myself
    live = slot_ids < tile_counts[0]
    wanted_hit = (home[None, :] == peer_ids[:, None]) & (remote & live)[None, :]
    slot_of = jnp.max(jnp.where(wanted_hit, slot_ids[None, :], -1), axis=1)
    wanted = jnp.max(jnp.where(wanted_hit, (col_blocks % local_blocks)[None, :], -1), axis=1)
    asked = lax.all_to_all(wanted[:, None], "nodes", split_axis=0, concat_axis=0, tiled=True)[:, 0]
    blocks = features.reshape(local_blocks, block_rows, width_in)
    totals = aggregate(
        blocks, tile_values, row_local, col_blocks, home, remote, live, asked, slot_of, peers_total
    )
    aggregated = totals.reshape(local_blocks * block_rows, width_in).astype(jnp.bfloat16)
    preact = jnp.dot(aggregated, weight, preferred_element_type=jnp.float32)
    hidden = jax.nn.silu(preact).astype(jnp.bfloat16)
    sigma = jax.nn.sigmoid(preact)
    delta = (cotangent.astype(jnp.float32) * sigma * (1.0 + preact * (1.0 - sigma))).astype(
        jnp.bfloat16
    )
    local_grad = lax.dot_general(
        aggregated, delta, (((0,), (0,)), ((), ())), preferred_element_type=jnp.float32
    )
    node_total = peers_total * local_blocks * block_rows
    weight_grad = lax.psum(local_grad, "nodes") / jnp.sqrt(jnp.float32(node_total))
    upstream = lax.dot_general(
        delta, weight, (((1,), (1,)), ((), ())), preferred_element_type=jnp.float32
    ).astype(jnp.bfloat16)
    grad_blocks = upstream.reshape(local_blocks, block_rows, width_in)
    grad_totals = aggregate(
        grad_blocks,
        tile_values,
        row_local,
        col_blocks,
        home,
        remote,
        live,
        asked,
        slot_of,
        peers_total,
    )
    feature_grad = grad_totals.reshape(local_blocks * block_rows, width_in).astype(jnp.bfloat16)
    return (hidden, weight_grad, feature_grad)


def solution(mesh):
    return jax.shard_map(
        on_device,
        mesh=mesh,
        in_specs=(
            P("nodes", None),
            P(),
            P("nodes", None),
            P("nodes", None),
            P("nodes"),
            P("nodes", None, None),
        ),
        out_specs=(P("nodes", None), P(), P("nodes", None)),
        check_vma=False,
    )
```

profile of v0, /device:TPU:38, one launch (start us, length us, event | category | flops | bytes accessed | tf_op | source)
XLA Modules:
  0.0 803.4 jit_solution(978724783612101770)
XLA Ops:
  9.5 10.2 %all-to-all-start = ((s32[128,1,1]{2,1,0:T(1,128)}), s32[128,1,1]{2,1,0:T(1,128)S(1)}, u32[]{:S(2)}, u32[]{:S(2)}) async-start(s32[128,1,1]{2,1,0:T(1,128)} %copy.67), calls=%async_computation | async-start | bytes 131072 | tf_op jit(solution)/shard_map/all_to_all | solution.py:65
  26.7 15.6 %fusion.59 = (bf16[96,256,128]{1,2,0:T(8,128)(2,1)}, f32[96,256,128]{1,2,0:T(8,128)}) fusion(bf16[96,256,256]{2,1,0:T(8,128)(2,1)} %param.19, bf16[96,256,128]{2,1,0:T(8,128)(2,1)} %gather_fusion.2, pred[96]{0:T(512)(128)(4,1)S(1)} %get-tuple-element.9), kind=kOutput, calls=%fused_computation.104 | convolution fusion | flops 1616904192 | bytes 37748832 | tf_op jit(solution)/shard_map/jab,jaf->jbf/dot_general | solution.py:12
  42.3 9.2 %gather_fusion.3 = bf16[128,256,128]{1,2,0:T(8,128)(2,1)} fusion(bf16[96,256,128]{1,2,0:T(8,128)(2,1)} %get-tuple-element.23, s32[1024]{0:T(1024)S(1)} %pad_clamp_fusion), kind=kCustom, calls=%fused_computation.3.clone | custom fusion | bytes 16777728 | tf_op jit(solution)/shard_map/jit(_take)/gather | solution.py:18
  59.1 10.7 %all-to-all-start.2 = ((bf16[128,256,128]{1,2,0:T(8,128)(2,1)}), bf16[128,256,128]{1,2,0:T(8,128)(2,1)}, u32[]{:S(2)}, u32[]{:S(2)}) async-start(bf16[128,256,128]{1,2,0:T(8,128)(2,1)} %select_select_fusion.2), calls=%async_computation.2 | async-start | bytes 16777216 | tf_op jit(solution)/shard_map/all_to_all | solution.py:31
  78.5 11.9 %copy.68 = bf16[128,256,128]{1,2,0:T(8,128)(2,1)} copy(bf16[128,256,128]{2,1,0:T(8,128)(2,1)} %gather_fusion) | data formatting | bytes 16777216 | tf_op jit(solution)/shard_map/jit(_take)/gather | solution.py:23
  100.3 72.2 %all-to-all-done.2 = bf16[128,256,128]{1,2,0:T(8,128)(2,1)} async-done(((bf16[128,256,128]{1,2,0:T(8,128)(2,1)}), bf16[128,256,128]{1,2,0:T(8,128)(2,1)}, u32[]{:S(2)}, u32[]{:S(2)}) %all-to-all-start.2) | async-done | bytes 8388640 | tf_op jit(solution)/shard_map/all_to_all | solution.py:31
  172.6 8.9 %all-to-all-start.1 = ((bf16[128,256,128]{1,2,0:T(8,128)(2,1)}), bf16[128,256,128]{1,2,0:T(8,128)(2,1)}, u32[]{:S(2)}, u32[]{:S(2)}) async-start(bf16[128,256,128]{1,2,0:T(8,128)(2,1)} %select_select_fusion.3), calls=%async_computation.1 | async-start | bytes 16777216 | tf_op jit(solution)/shard_map/all_to_all | solution.py:26
  181.7 12.7 %copy.72 = f32[96,256,128]{2,0,1:T(8,128)} copy(f32[96,256,128]{1,2,0:T(8,128)} %get-tuple-element.24) | data formatting | bytes 25165824 | tf_op jit(solution)/shard_map/jab,jaf->jbf/dot_general | solution.py:12
  194.4 12.4 %copy.73 = bf16[128,256,128]{2,0,1:T(8,128)(2,1)} copy(bf16[128,256,128]{1,2,0:T(8,128)(2,1)} %all-to-all-done.2) | data formatting | bytes 16777216 | tf_op jit(solution)/shard_map/all_to_all | solution.py:31
  206.8 77.5 %all-to-all-done.1 = bf16[128,256,128]{1,2,0:T(8,128)(2,1)} async-done(((bf16[128,256,128]{1,2,0:T(8,128)(2,1)}), bf16[128,256,128]{1,2,0:T(8,128)(2,1)}, u32[]{:S(2)}, u32[]{:S(2)}) %all-to-all-start.1) | async-done | bytes 8388640 | tf_op jit(solution)/shard_map/all_to_all | solution.py:26
  291.8 9.6 %gather_fusion.1 = bf16[96,256,128]{1,2,0:T(8,128)(2,1)} fusion(bf16[136,256,128]{1,2,0:T(8,128)(2,1)} %pad_maximum_fusion, s32[1024]{0:T(1024)S(1)} %pad_clamp_fusion.2), kind=kCustom, calls=%fused_computation.1.clone | custom fusion | bytes 12583296 | tf_op jit(solution)/shard_map/jit(_take)/gather | solution.py:29
  301.3 16.0 %fusion.12 = f32[96,256,128]{1,2,0:T(8,128)} fusion(bf16[96,256,256]{2,1,0:T(8,128)(2,1)} %param.19, bf16[96,256,128]{1,2,0:T(8,128)(2,1)} %gather_fusion.1, pred[96]{0:T(512)(128)(4,1)S(1)} %get-tuple-element.17), kind=kOutput, calls=%fused_computation.26 | convolution fusion | flops 1613758464 | bytes 31457376 | tf_op jit(solution)/shard_map/jab,jbf->jaf/dot_general | solution.py:30
  317.3 12.7 %copy.70 = f32[96,256,128]{2,0,1:T(8,128)} copy(f32[96,256,128]{1,2,0:T(8,128)} %fusion.12) | data formatting | bytes 25165824 | tf_op jit(solution)/shard_map/jab,jbf->jaf/dot_general | solution.py:30
  355.3 11.9 %copy.75 = bf16[128,256,128]{1,2,0:T(8,128)(2,1)} copy(bf16[128,256,128]{2,1,0:T(8,128)(2,1)} %gather_fusion.4) | data formatting | bytes 16777216 | tf_op jit(solution)/shard_map/jit(_take)/gather | solution.py:23
  389.2 15.5 %fusion.60 = (bf16[96,256,128]{1,2,0:T(8,128)(2,1)}, f32[96,256,128]{1,2,0:T(8,128)}) fusion(bf16[96,256,256]{2,1,0:T(8,128)(2,1)} %param.19, bf16[96,256,128]{2,1,0:T(8,128)(2,1)} %gather_fusion.6, pred[96]{0:T(512)(128)(4,1)S(1)} %get-tuple-element.9), kind=kOutput, calls=%fused_computation.105 | convolution fusion | flops 1616904192 | bytes 37748832 | tf_op jit(solution)/shard_map/jab,jaf->jbf/dot_general | solution.py:12
  404.7 9.3 %gather_fusion.7 = bf16[128,256,128]{1,2,0:T(8,128)(2,1)} fusion(bf16[96,256,128]{1,2,0:T(8,128)(2,1)} %get-tuple-element.25, s32[1024]{0:T(1024)S(1)} %pad_clamp_fusion), kind=kCustom, calls=%fused_computation.7.clone | custom fusion | bytes 16777728 | tf_op jit(solution)/shard_map/jit(_take)/gather | solution.py:18
  421.6 64.9 %all-to-all-done.3 = bf16[128,256,128]{1,2,0:T(8,128)(2,1)} async-done(((bf16[128,256,128]{1,2,0:T(8,128)(2,1)}), bf16[128,256,128]{1,2,0:T(8,128)(2,1)}, u32[]{:S(2)}, u32[]{:S(2)}) %all-to-all-start.3) | async-done | bytes 8388640 | tf_op jit(solution)/shard_map/all_to_all | solution.py:26
  486.6 9.3 %all-to-all-start.4 = ((bf16[128,256,128]{1,2,0:T(8,128)(2,1)}), bf16[128,256,128]{1,2,0:T(8,128)(2,1)}, u32[]{:S(2)}, u32[]{:S(2)}) async-start(bf16[128,256,128]{1,2,0:T(8,128)(2,1)} %select_select_fusion), calls=%async_computation.4 | async-start | bytes 16777216 | tf_op jit(solution)/shard_map/all_to_all | solution.py:31
  497.2 12.7 %copy.79 = f32[96,256,128]{2,0,1:T(8,128)} copy(f32[96,256,128]{1,2,0:T(8,128)} %get-tuple-element.26) | data formatting | bytes 25165824 | tf_op jit(solution)/shard_map/jab,jaf->jbf/dot_general | solution.py:12
  509.9 207.3 %all-reduce.2.cloned.1.call-done = f32[128,256]{1,0:T(8,128)} async-done(((f32[128,256]{1,0:T(8,128)}), f32[128,256]{1,0:T(8,128)}) %all-reduce.2.cloned.1.call-update) | async-done | bytes 131088 | tf_op jit(solution)/shard_map/psum | solution.py:81
  726.1 9.6 %gather_fusion.5 = bf16[96,256,128]{1,2,0:T(8,128)(2,1)} fusion(bf16[136,256,128]{1,2,0:T(8,128)(2,1)} %pad_maximum_fusion.1, s32[1024]{0:T(1024)S(1)} %pad_clamp_fusion.2), kind=kCustom, calls=%fused_computation.5.clone | custom fusion | bytes 12583296 | tf_op jit(solution)/shard_map/jit(_take)/gather | solution.py:29
  735.7 16.0 %fusion.18 = f32[96,256,128]{1,2,0:T(8,128)} fusion(bf16[96,256,256]{2,1,0:T(8,128)(2,1)} %param.19, bf16[96,256,128]{1,2,0:T(8,128)(2,1)} %gather_fusion.5, pred[96]{0:T(512)(128)(4,1)S(1)} %get-tuple-element.17), kind=kOutput, calls=%fused_computation.28 | convolution fusion | flops 1613758464 | bytes 31457376 | tf_op jit(solution)/shard_map/jab,jbf->jaf/dot_general | solution.py:30
  751.7 12.7 %copy.77 = f32[96,256,128]{2,0,1:T(8,128)} copy(f32[96,256,128]{1,2,0:T(8,128)} %fusion.18) | data formatting | bytes 25165824 | tf_op jit(solution)/shard_map/jab,jbf->jaf/dot_general | solution.py:30
  778.5 12.4 %copy.80 = bf16[128,256,128]{2,0,1:T(8,128)(2,1)} copy(bf16[128,256,128]{1,2,0:T(8,128)(2,1)} %all-to-all-done.4) | data formatting | bytes 16777216 | tf_op jit(solution)/shard_map/all_to_all | solution.py:31
  (61 shorter events, 127.2 us)
Async XLA Ops:
  7.2 339.1 %copy-start = (bf16[128,256]{1,0:T(8,128)(2,1)S(1)}, bf16[128,256]{1,0:T(8,128)(2,1)}, u32[]{:S(2)}) copy-start(bf16[128,256]{1,0:T(8,128)(2,1)} %param.15) | copy-start | bytes 196612
  9.5 49.5 %all-to-all-start = ((s32[128,1,1]{2,1,0:T(1,128)}), s32[128,1,1]{2,1,0:T(1,128)S(1)}, u32[]{:S(2)}, u32[]{:S(2)}) async-start(s32[128,1,1]{2,1,0:T(1,128)} %copy.67), calls=%async_computation | async-start | bytes 131072 | tf_op jit(solution)/shard_map/all_to_all | solution.py:65
  59.1 13.1 %copy-start.2 = (bf16[2048,128]{1,0:T(8,128)(2,1)S(1)}, bf16[2048,128]{1,0:T(8,128)(2,1)}, u32[]{:S(2)}) copy-start(bf16[2048,128]{1,0:T(8,128)(2,1)} %param.14) | copy-start | bytes 1572868
  59.1 113.5 %all-to-all-start.2 = ((bf16[128,256,128]{1,2,0:T(8,128)(2,1)}), bf16[128,256,128]{1,2,0:T(8,128)(2,1)}, u32[]{:S(2)}, u32[]{:S(2)}) async-start(bf16[128,256,128]{1,2,0:T(8,128)(2,1)} %select_select_fusion.2), calls=%async_computation.2 | async-start | bytes 16777216 | tf_op jit(solution)/shard_map/all_to_all | solution.py:31
  172.6 111.7 %all-to-all-start.1 = ((bf16[128,256,128]{1,2,0:T(8,128)(2,1)}), bf16[128,256,128]{1,2,0:T(8,128)(2,1)}, u32[]{:S(2)}, u32[]{:S(2)}) async-start(bf16[128,256,128]{1,2,0:T(8,128)(2,1)} %select_select_fusion.3), calls=%async_computation.1 | async-start | bytes 16777216 | tf_op jit(solution)/shard_map/all_to_all | solution.py:26
  181.7 12.7 %copy-start.3 = (s32[96,2]{0,1:T(2,128)S(1)}, s32[96,2]{0,1:T(2,128)}, u32[]{:S(2)}) copy-start(s32[96,2]{0,1:T(2,128)} %param.17) | copy-start | bytes 2308
  330.0 14.9 %slice-start = ((s8[8388608]{0:T(1024)(128)(4,1)}), s8[4194304]{0:T(1024)(128)(4,1)S(1)}, s32[]{:S(2)}) async-start(s8[8388608]{0:T(1024)(128)(4,1)} %bitcast.70), calls=%async_computation.6 | async-start | bytes 8388608
  337.2 7.8 slice-start.1
  344.9 1.3 copy-start.4
  374.8 111.8 %all-to-all-start.3 = ((bf16[128,256,128]{1,2,0:T(8,128)(2,1)}), bf16[128,256,128]{1,2,0:T(8,128)(2,1)}, u32[]{:S(2)}, u32[]{:S(2)}) async-start(bf16[128,256,128]{1,2,0:T(8,128)(2,1)} %select_select_fusion.1), calls=%async_computation.3 | async-start | bytes 16777216 | tf_op jit(solution)/shard_map/all_to_all | solution.py:26
  486.6 291.9 %all-to-all-start.4 = ((bf16[128,256,128]{1,2,0:T(8,128)(2,1)}), bf16[128,256,128]{1,2,0:T(8,128)(2,1)}, u32[]{:S(2)}, u32[]{:S(2)}) async-start(bf16[128,256,128]{1,2,0:T(8,128)(2,1)} %select_select_fusion), calls=%async_computation.4 | async-start | bytes 16777216 | tf_op jit(solution)/shard_map/all_to_all | solution.py:31
  495.9 221.3 %all-reduce.2.cloned.1.call-start = ((), (), s32[]{:S(2)}) async-start(), calls=%async_computation.5 | async-start | bytes 262144 | tf_op jit(solution)/shard_map/psum | solution.py:81
  778.5 17.9 %copy-start.1 = (bf16[128,256]{1,0:T(8,128)(2,1)S(1)}, bf16[128,256]{1,0:T(8,128)(2,1)}, u32[]{:S(2)}) copy-start(bf16[128,256]{1,0:T(8,128)(2,1)} %param.15) | copy-start | bytes 196612
Sparse Core Ops, SparseCore 0:
  502.0 215.0 all-reduce.1
where the time goes:
time: 814 us; the launch traced here: 803 us
  waiting for transfers between devices  422 us (52%)
  local copies, waits for them, and re-layouts  165 us (20%)
  matrix products  101 us (12%)
  other arithmetic  52.4 us (6%)
  starting transfers between devices  47.6 us (6%)
  between operations  15.2 us (2%)
    psum x1, waiting for transfers between devices, on_device(): lax.psum(local_grad, 'nodes') / jnp.sqrt(jnp.float32(node_total))  207 us
    all_to_all x2, waiting for transfers between devices, aggregate(): lax.all_to_all(sending, 'nodes', split_axis=0, concat_axis=0, tiled=True)  142 us
    all_to_all x2, waiting for transfers between devices, aggregate(): lax.all_to_all(outgoing, 'nodes', split_axis=0, concat_axis=0, tiled=True)  72.2 us
    gather x4, local copies, waits for them, and re-layouts, aggregate(): jnp.take(blocks, jnp.maximum(asked, 0), axis=0)  36.7 us
    dot_general x2, matrix products, aggregate(): jnp.einsum('jab,jbf->jaf', tile_values, fetched, preferred_element_type=j...  32 us
    dot_general x2, matrix products, aggregate(): jnp.einsum('jab,jaf->jbf', tile_values, own_rows, preferred_element_type=...  31.1 us
    dot_general x2, local copies, waits for them, and re-layouts, aggregate(): jnp.einsum('jab,jaf->jbf', tile_values, own_rows, preferred_element_type=...  25.4 us
    dot_general x2, local copies, waits for them, and re-layouts, aggregate(): jnp.einsum('jab,jbf->jaf', tile_values, fetched, preferred_element_type=j...  25.3 us
  transfers between devices with their start and end apart: 6, of which 4 were waited for; matrix products, arithmetic and copies ran while one was open for 26% of the time, Pallas kernels for 0%

commit v1 on v0

v1 whole, which is shorter than its diff:
```python
import functools
import math

import jax
import jax.numpy as jnp
from jax import lax
from jax.experimental import pallas as pl
from jax.experimental.pallas import tpu as pltpu
from jax.sharding import PartitionSpec as P

VMEM_LIMIT = 60 * 1024 * 1024
GROUP = 16
PARTS = 4
EXTRA = 16
TWICE = 64


def whole(*shape):
    return pl.BlockSpec(shape, lambda *_: (0,) * len(shape), pipeline_mode=pl.Buffered(1))


def params(limit=VMEM_LIMIT):
    return pltpu.CompilerParams(vmem_limit_bytes=limit)


def send_blocks(asked_ref, blocks_ref, out_ref, sems):
    def copy(q):
        block = jnp.maximum(asked_ref[q], 0)
        return pltpu.make_async_copy(blocks_ref.at[block], out_ref.at[q], sems.at[q])

    def start(q, carry):
        @pl.when(asked_ref[q] >= 0)
        def _():
            copy(q).start()

        return carry

    def wait(q, carry):
        @pl.when(asked_ref[q] >= 0)
        def _():
            copy(q).wait()

        return carry

    peers = asked_ref.shape[0]
    lax.fori_loop(0, peers, start, 0)
    lax.fori_loop(0, peers, wait, 0)


def pick(asked, blocks):
    peers = asked.shape[0]
    locals_, rows, width = blocks.shape
    return pl.pallas_call(
        send_blocks,
        grid_spec=pltpu.PrefetchScalarGridSpec(
            num_scalar_prefetch=1,
            grid=(1,),
            in_specs=[whole(locals_, rows, width)],
            out_specs=pl.BlockSpec(memory_space=pl.ANY),
            scratch_shapes=[pltpu.SemaphoreType.DMA((peers,))],
        ),
        out_shape=jax.ShapeDtypeStruct((peers, rows, width), blocks.dtype),
        compiler_params=params(),
    )(asked, blocks)


def transposed_kernel(
    peers, row_ref, dest_ref, again_ref, blocks_ref, tiles_ref, out_ref, total_ref
):
    step = pl.program_id(0)

    @pl.when(step == 0)
    def _():
        total_ref[...] = jnp.zeros_like(total_ref)

    def visit(at, carry):
        slot = step * GROUP + at
        dest = dest_ref[slot]

        @pl.when(dest >= 0)
        def _():
            row = row_ref[slot]
            product = lax.dot_general(
                tiles_ref[at],
                blocks_ref[row],
                (((0,), (0,)), ((), ())),
                preferred_element_type=jnp.float32,
            )
            remote = dest < peers

            @pl.when(remote & (again_ref[slot] == 0))
            def _():
                out_ref[dest] = product.astype(out_ref.dtype)

            @pl.when(remote & (again_ref[slot] == 1))
            def _():
                out_ref[dest] = (out_ref[dest].astype(jnp.float32) + product).astype(out_ref.dtype)

            @pl.when(jnp.logical_not(remote))
            def _():
                column = dest - peers
                total_ref[column] += product
                total_ref[row] += jnp.dot(
                    tiles_ref[at], blocks_ref[column], preferred_element_type=jnp.float32
                )

        return carry

    lax.fori_loop(0, GROUP, visit, 0)


def transposed_products(row_local, dest, again, blocks, tile_values, peers):
    slots, rows, _ = tile_values.shape
    locals_, _, width = blocks.shape
    return pl.pallas_call(
        functools.partial(transposed_kernel, peers),
        grid_spec=pltpu.PrefetchScalarGridSpec(
            num_scalar_prefetch=3,
            grid=(slots // GROUP,),
            in_specs=[
                whole(locals_, rows, width),
                pl.BlockSpec((GROUP, rows, rows), lambda i, *_: (i, 0, 0)),
            ],
            out_specs=[whole(peers, rows, width), whole(locals_, rows, width)],
        ),
        out_shape=[
            jax.ShapeDtypeStruct((peers, rows, width), blocks.dtype),
            jax.ShapeDtypeStruct((locals_, rows, width), jnp.float32),
        ],
        compiler_params=params(),
        cost_estimate=pl.CostEstimate(
            flops=3 * slots * rows * rows * width, bytes_accessed=24 << 20, transcendentals=0
        ),
    )(row_local, dest, again, blocks, tile_values)


def direct_kernel(peers, row_ref, dest_ref, arrived_ref, tiles_ref, start_ref, total_ref):
    step = pl.program_id(0)

    @pl.when(step == 0)
    def _():
        total_ref[...] = start_ref[...]

    def visit(at, carry):
        slot = step * GROUP + at
        source = dest_ref[slot]

        @pl.when((source >= 0) & (source < peers))
        def _():
            total_ref[row_ref[slot]] += jnp.dot(
                tiles_ref[at], arrived_ref[source], preferred_element_type=jnp.float32
            )

        return carry

    lax.fori_loop(0, GROUP, visit, 0)


def direct_products(row_local, dest, arrived, tile_values, start):
    slots, rows, _ = tile_values.shape
    peers, _, width = arrived.shape
    locals_ = start.shape[0]
    return pl.pallas_call(
        functools.partial(direct_kernel, peers),
        grid_spec=pltpu.PrefetchScalarGridSpec(
            num_scalar_prefetch=2,
            grid=(slots // GROUP,),
            in_specs=[
                whole(peers, rows, width),
                pl.BlockSpec((GROUP, rows, rows), lambda i, *_: (i, 0, 0)),
                whole(locals_, rows, width),
            ],
            out_specs=whole(locals_, rows, width),
        ),
        out_shape=jax.ShapeDtypeStruct((locals_, rows, width), jnp.float32),
        compiler_params=params(),
        cost_estimate=pl.CostEstimate(
            flops=2 * slots * rows * rows * width, bytes_accessed=24 << 20, transcendentals=0
        ),
    )(row_local, dest, arrived, tile_values, start)


def add_returned(asked_ref, returned_ref, start_ref, total_ref, landed_ref, sems):
    def copy(q):
        return pltpu.make_async_copy(returned_ref.at[q], landed_ref.at[q], sems.at[q])

    def start(q, carry):
        @pl.when(asked_ref[q] >= 0)
        def _():
            copy(q).start()

        return carry

    def add(q, carry):
        block = asked_ref[q]

        @pl.when(block >= 0)
        def _():
            copy(q).wait()
            total_ref[block] += landed_ref[q].astype(jnp.float32)

        return carry

    peers = asked_ref.shape[0]
    lax.fori_loop(0, peers, start, 0)
    total_ref[...] = start_ref[...]
    lax.fori_loop(0, peers, add, 0)


def dense_kernel(
    asked_ref,
    returned_ref,
    start_ref,
    weight_ref,
    cotangent_ref,
    hidden_ref,
    grad_ref,
    upstream_ref,
    out_ref,
    total_ref,
    landed_ref,
    sems,
):
    add_returned(asked_ref, returned_ref, start_ref, total_ref, landed_ref, sems)
    grad_ref[...] = jnp.zeros_like(grad_ref)
    weight = weight_ref[...]

    def block_step(k, carry):
        aggregated = total_ref[k].astype(jnp.bfloat16)
        preact = jnp.dot(aggregated, weight, preferred_element_type=jnp.float32)
        sigma = 1.0 / (1.0 + jnp.exp(-preact))
        hidden_ref[k] = (preact * sigma).astype(jnp.bfloat16)
        delta = (
            cotangent_ref[k].astype(jnp.float32) * sigma * (1.0 + preact * (1.0 - sigma))
        ).astype(jnp.bfloat16)
        grad_ref[...] += lax.dot_general(
            aggregated, delta, (((0,), (0,)), ((), ())), preferred_element_type=jnp.float32
        )
        upstream_ref[k] = lax.dot_general(
            delta, weight, (((1,), (1,)), ((), ())), preferred_element_type=jnp.float32
        ).astype(jnp.bfloat16)
        return carry

    lax.fori_loop(0, total_ref.shape[0], block_step, 0)
    send_blocks(asked_ref, upstream_ref, out_ref, sems)


def dense(asked, returned, start, weight, cotangent):
    peers, rows, width = returned.shape
    locals_ = start.shape[0]
    hid = weight.shape[1]
    return pl.pallas_call(
        dense_kernel,
        grid_spec=pltpu.PrefetchScalarGridSpec(
            num_scalar_prefetch=1,
            grid=(1,),
            in_specs=[
                pl.BlockSpec(memory_space=pl.ANY),
                whole(locals_, rows, width),
                whole(width, hid),
                whole(locals_, rows, hid),
            ],
            out_specs=[
                whole(locals_, rows, hid),
                whole(width, hid),
                whole(locals_, rows, width),
                pl.BlockSpec(memory_space=pl.ANY),
            ],
            scratch_shapes=[
                pltpu.VMEM((locals_, rows, width), jnp.float32),
                pltpu.VMEM((peers, rows, width), returned.dtype),
                pltpu.SemaphoreType.DMA((peers,)),
            ],
        ),
        out_shape=[
            jax.ShapeDtypeStruct((locals_, rows, hid), jnp.bfloat16),
            jax.ShapeDtypeStruct((width, hid), jnp.float32),
            jax.ShapeDtypeStruct((locals_, rows, width), jnp.bfloat16),
            jax.ShapeDtypeStruct((peers, rows, width), jnp.bfloat16),
        ],
        compiler_params=params(),
    )(asked, returned, start, weight, cotangent)


def finish_kernel(asked_ref, returned_ref, start_ref, out_ref, total_ref, landed_ref, sems):
    add_returned(asked_ref, returned_ref, start_ref, total_ref, landed_ref, sems)
    out_ref[...] = total_ref[...].astype(out_ref.dtype)


def finish(asked, returned, start):
    peers, rows, width = returned.shape
    locals_ = start.shape[0]
    return pl.pallas_call(
        finish_kernel,
        grid_spec=pltpu.PrefetchScalarGridSpec(
            num_scalar_prefetch=1,
            grid=(1,),
            in_specs=[pl.BlockSpec(memory_space=pl.ANY), whole(locals_, rows, width)],
            out_specs=whole(locals_, rows, width),
            scratch_shapes=[
                pltpu.VMEM((locals_, rows, width), jnp.float32),
                pltpu.VMEM((peers, rows, width), returned.dtype),
                pltpu.SemaphoreType.DMA((peers,)),
            ],
        ),
        out_shape=jax.ShapeDtypeStruct((locals_, rows, width), jnp.bfloat16),
        compiler_params=params(),
    )(asked, returned, start)


def exchange(values):
    return lax.all_to_all(values, "nodes", split_axis=0, concat_axis=0, tiled=True)


ASKED, VIA, RELAYED, CAME_VIA, WANTED, FITS = range(6)
OPEN = -2


def plan_kernel(me_ref, wanted_ref, plan_ref, free_ref, rows_ref, columns_ref):
    peers = wanted_ref.shape[0]
    me = me_ref[0]
    raw = wanted_ref[...]
    u_ids = lax.broadcasted_iota(jnp.int32, raw.shape, 0)
    v_ids = lax.broadcasted_iota(jnp.int32, raw.shape, 1)
    named = (raw >= 0).astype(jnp.float32)
    flipped = named.T
    skewed = flipped
    for bit in range(peers.bit_length() - 1):
        turned = pltpu.roll(skewed, peers - (1 << bit), 1)
        skewed = jnp.where(((u_ids >> bit) & 1) == 1, turned, skewed)
    free_ref[...] = (1.0 - skewed.T).astype(jnp.int32)
    route = jnp.where((named > 0) & (flipped > 0), OPEN, -1)
    spare = 1 - flipped.astype(jnp.int32)

    def left_open(route):
        return jnp.sum((route == OPEN).astype(jnp.float32)).astype(jnp.int32)

    def one(turn, carry):
        route, spare = carry
        fits = (route == OPEN) & ((spare & free_ref[pl.ds(turn, 1), :]) > 0)
        first = jnp.min(jnp.where(fits, u_ids, peers), axis=0, keepdims=True)
        chosen = fits & (u_ids == first)
        route = jnp.where(chosen, (v_ids + turn) & (peers - 1), route)
        spare = jnp.where(chosen, 0, spare)
        return route, pltpu.roll(spare, peers - 1, 1)

    def some(carry):
        turn, _, route, spare = carry
        route, spare = lax.fori_loop(0, 8, lambda i, c: one(turn + i, c), (route, spare))
        return turn + 8, left_open(route), route, spare

    _, left, route, _ = lax.while_loop(
        lambda carry: (carry[0] < peers) & (carry[1] > 0),
        some,
        (jnp.int32(0), left_open(route), route, spare),
    )
    rows_ref[...] = route
    columns_ref[...] = route.astype(jnp.float32).T.astype(jnp.int32)
    plan_ref[VIA : VIA + 1, :] = rows_ref[pl.ds(me, 1), :]
    plan_ref[CAME_VIA : CAME_VIA + 1, :] = columns_ref[pl.ds(me, 1), :]
    plan_ref[RELAYED : RELAYED + 1, :] = jnp.max(
        jnp.where(route == me, u_ids, -1), axis=0, keepdims=True
    )
    columns_ref[...] = raw.astype(jnp.float32).T.astype(jnp.int32)
    plan_ref[ASKED : ASKED + 1, :] = columns_ref[pl.ds(me, 1), :]
    plan_ref[WANTED : WANTED + 1, :] = wanted_ref[pl.ds(me, 1), :]
    twice = jnp.sum((raw >= TWICE).astype(jnp.float32)).astype(jnp.int32)
    fits = jnp.where((left == 0) & (twice == 0), 1, 0)
    plan_ref[FITS:, :] = jnp.full((plan_ref.shape[0] - FITS, peers), fits, jnp.int32)


def make_plan(myself, wanted):
    peers = wanted.shape[0]
    square = pltpu.VMEM((peers, peers), jnp.int32)
    return pl.pallas_call(
        plan_kernel,
        grid_spec=pltpu.PrefetchScalarGridSpec(
            num_scalar_prefetch=1,
            grid=(1,),
            in_specs=[whole(peers, peers)],
            out_specs=whole(8, peers),
            scratch_shapes=[square, square, square],
        ),
        out_shape=jax.ShapeDtypeStruct((8, peers), jnp.int32),
        compiler_params=params(),
    )(jnp.full((1,), myself, jnp.int32), wanted)


def each_peer(peers, act):
    def step(q, carry):
        act(q)
        return carry

    lax.fori_loop(0, peers, step, 0, unroll=8)


def send_first(plan_ref, blocks_ref, out_ref, sems):
    peers = plan_ref.shape[1]
    half = blocks_ref.shape[1] // 2

    def direct(q):
        block = jnp.maximum(plan_ref[ASKED, q], 0)
        return pltpu.make_async_copy(
            blocks_ref.at[block, pl.ds(0, half)], out_ref.at[q, pl.ds(0, half)], sems.at[q]
        )

    def relayed(q):
        block = jnp.maximum(plan_ref[ASKED, q], 0)
        via = jnp.maximum(plan_ref[VIA, q], 0)
        return pltpu.make_async_copy(
            blocks_ref.at[block, pl.ds(half, half)],
            out_ref.at[via, pl.ds(0, half)],
            sems.at[peers + q],
        )

    def start(q):
        @pl.when(plan_ref[ASKED, q] >= 0)
        def _():
            direct(q).start()

        @pl.when(plan_ref[VIA, q] >= 0)
        def _():
            relayed(q).start()

    def wait(q):
        @pl.when(plan_ref[ASKED, q] >= 0)
        def _():
            direct(q).wait()

        @pl.when(plan_ref[VIA, q] >= 0)
        def _():
            relayed(q).wait()

    each_peer(peers, start)
    each_peer(peers, wait)


def first_halves(plan, blocks):
    peers = plan.shape[1]
    locals_, rows, width = blocks.shape
    return pl.pallas_call(
        send_first,
        grid_spec=pltpu.PrefetchScalarGridSpec(
            num_scalar_prefetch=1,
            grid=(1,),
            in_specs=[whole(locals_, rows, width)],
            out_specs=pl.BlockSpec(memory_space=pl.ANY),
            scratch_shapes=[pltpu.SemaphoreType.DMA((2 * peers,))],
        ),
        out_shape=jax.ShapeDtypeStruct((peers, rows // 2, width), blocks.dtype),
        compiler_params=params(),
    )(plan, blocks)


def tiles_spec(rows):
    return pl.BlockSpec(
        (GROUP, rows, rows), lambda i, plan, slots: (jnp.minimum(i, slots[3, 0]), 0, 0)
    )


ROW, HOME, COLUMN, LAST = range(4)


def products_kernel(plan_ref, slots_ref, blocks_ref, tiles_ref, out_ref, total_ref):
    step = pl.program_id(0)
    peers = plan_ref.shape[1]
    rows = blocks_ref.shape[1]
    half = rows // 2
    locals_ = blocks_ref.shape[0]

    @pl.when(step == 0)
    def _():
        total_ref[...] = jnp.zeros_like(total_ref)

        def second_half(q):
            @pl.when((plan_ref[ASKED, q] >= 0) & (plan_ref[WANTED, q] < 0))
            def _():
                out_ref[q, pl.ds(0, half)] = blocks_ref[plan_ref[ASKED, q], pl.ds(half, half)]

        each_peer(peers, second_half)

    @pl.when(step <= slots_ref[LAST, 0])
    def _():
        for at in range(GROUP):
            slot = step * GROUP + at
            row, home, column = slots_ref[ROW, slot], slots_ref[HOME, slot], slots_ref[COLUMN, slot]
            tile = tiles_ref[at]
            product = lax.dot_general(
                tile, blocks_ref[row], (((0,), (0,)), ((), ())), preferred_element_type=jnp.float32
            )
            out_ref[home, pl.ds(0, rows)] = product.astype(out_ref.dtype)

            @pl.when(column < locals_)
            def _():
                total_ref[column] += product
                total_ref[row] += jnp.dot(
                    tile, blocks_ref[column], preferred_element_type=jnp.float32
                )


def own_products(plan, slots, blocks, tile_values, extra):
    peers = plan.shape[1]
    slot_total, rows, _ = tile_values.shape
    locals_, _, width = blocks.shape
    return pl.pallas_call(
        products_kernel,
        grid_spec=pltpu.PrefetchScalarGridSpec(
            num_scalar_prefetch=2,
            grid=(slot_total // GROUP,),
            in_specs=[whole(locals_, rows, width), tiles_spec(rows)],
            out_specs=[whole(peers, rows + extra, width), whole(locals_, rows, width)],
        ),
        out_shape=[
            jax.ShapeDtypeStruct((peers, rows + extra, width), blocks.dtype),
            jax.ShapeDtypeStruct((locals_, rows, width), jnp.float32),
        ],
        compiler_params=params(),
        cost_estimate=pl.CostEstimate(
            flops=3 * slot_total * rows * rows * width, bytes_accessed=24 << 20, transcendentals=0
        ),
    )(plan, slots, blocks, tile_values)


def three_parts(value):
    high = value.astype(jnp.bfloat16)
    rest = value - high.astype(jnp.float32)
    middle = rest.astype(jnp.bfloat16)
    low = (rest - middle.astype(jnp.float32)).astype(jnp.bfloat16)
    return [part.astype(jnp.float32) for part in (high, middle, low)]


def relay_kernel(plan_ref, came_ref, _, out_ref, held_ref, sems, *grad_refs):
    peers = plan_ref.shape[1]
    half = came_ref.shape[1] - (EXTRA if grad_refs else 0)

    def take(q):
        source = jnp.maximum(plan_ref[RELAYED, q], 0)
        return pltpu.make_async_copy(
            came_ref.at[source, pl.ds(0, half)], held_ref.at[q], sems.at[q]
        )

    def give(q):
        return pltpu.make_async_copy(
            held_ref.at[q], out_ref.at[q, pl.ds(half, half)], sems.at[peers + q]
        )

    def start(q):
        @pl.when(plan_ref[RELAYED, q] >= 0)
        def _():
            take(q).start()

    def turn(q):
        @pl.when(plan_ref[RELAYED, q] >= 0)
        def _():
            take(q).wait()
            give(q).start()

    def wait(q):
        @pl.when(plan_ref[RELAYED, q] >= 0)
        def _():
            give(q).wait()

    if grad_refs:
        (staged_ref,) = grad_refs
        bring = pltpu.make_async_copy(
            came_ref.at[:, pl.ds(half, EXTRA)], staged_ref, sems.at[2 * peers]
        )
        bring.start()
    each_peer(peers, start)
    if grad_refs:
        bring.wait()
        sums = jnp.sum(staged_ref[...].astype(jnp.float32), axis=0)
        own = (sums[4:6] + sums[2:4]) + sums[0:2]
        parts = three_parts(own)
        packed = jnp.concatenate(parts + [jnp.zeros((EXTRA - 6, own.shape[1]), jnp.float32)], 0)
        staged_ref[...] = jnp.broadcast_to(packed[None], staged_ref.shape).astype(jnp.bfloat16)
        put = pltpu.make_async_copy(
            staged_ref, out_ref.at[:, pl.ds(2 * half, EXTRA)], sems.at[2 * peers + 1]
        )
        put.start()
    each_peer(peers, turn)
    if grad_refs:
        put.wait()
    each_peer(peers, wait)


def relay(plan, came, outgoing, with_grad):
    peers, _, width = came.shape
    scratch = [
        pltpu.VMEM((peers, came.shape[1] - (EXTRA if with_grad else 0), width), came.dtype),
        pltpu.SemaphoreType.DMA((2 * peers + 2,)),
    ]
    if with_grad:
        scratch.append(pltpu.VMEM((peers, EXTRA, width), jnp.bfloat16))
    anywhere = pl.BlockSpec(memory_space=pl.ANY)
    return pl.pallas_call(
        relay_kernel,
        grid_spec=pltpu.PrefetchScalarGridSpec(
            num_scalar_prefetch=1,
            grid=(1,),
            in_specs=[anywhere, anywhere],
            out_specs=anywhere,
            scratch_shapes=scratch,
        ),
        out_shape=jax.ShapeDtypeStruct(outgoing.shape, outgoing.dtype),
        input_output_aliases={2: 0},
        compiler_params=params(),
    )(plan, came, outgoing)


def early_kernel(plan_ref, slots_ref, first_ref, tiles_ref, start_ref, total_ref, sums_ref):
    step = pl.program_id(0)
    half = tiles_ref.shape[2]
    locals_ = start_ref.shape[0]

    @pl.when(step == 0)
    def _():
        sums_ref[pl.ds(0, locals_)] = start_ref[...]

    @pl.when(step <= slots_ref[LAST, 0])
    def _():
        for at in range(GROUP):
            slot = step * GROUP + at
            remote = slots_ref[COLUMN, slot] == locals_
            row = jnp.where(remote, slots_ref[ROW, slot], locals_)
            sums_ref[row] += jnp.dot(
                tiles_ref[at],
                first_ref[slots_ref[HOME, slot], pl.ds(0, half)],
                preferred_element_type=jnp.float32,
            )

    @pl.when(step == pl.num_programs(0) - 1)
    def _():
        total_ref[...] = sums_ref[pl.ds(0, locals_)]


def early_products(plan, slots, first, tile_values, start):
    slot_total, rows, _ = tile_values.shape
    locals_, _, width = start.shape
    return pl.pallas_call(
        early_kernel,
        grid_spec=pltpu.PrefetchScalarGridSpec(
            num_scalar_prefetch=2,
            grid=(slot_total // GROUP,),
            in_specs=[
                whole(*first.shape),
                pl.BlockSpec(
                    (GROUP, rows, rows // 2),
                    lambda i, plan, slots: (jnp.minimum(i, slots[LAST, 0]), 0, 0),
                ),
                whole(*start.shape),
            ],
            out_specs=whole(*start.shape),
            scratch_shapes=[pltpu.VMEM((locals_ + 1, rows, width), jnp.float32)],
        ),
        out_shape=jax.ShapeDtypeStruct(start.shape, start.dtype),
        compiler_params=params(),
        cost_estimate=pl.CostEstimate(
            flops=slot_total * rows * rows * width, bytes_accessed=12 << 20, transcendentals=0
        ),
    )(plan, slots, first, tile_values, start)


def late_scratch(second, tile_values, start):
    peers, _, width = second.shape
    slot_total, rows, _ = tile_values.shape
    return [
        pltpu.VMEM((start.shape[0] + 1, rows, width), jnp.float32),
        pltpu.VMEM(second.shape, second.dtype),
        pltpu.VMEM((slot_total, rows, rows // 2), tile_values.dtype),
        pltpu.SemaphoreType.DMA((PARTS + slot_total // GROUP,)),
    ]


def late_sums(plan_ref, slots_ref, second_ref, tiles_ref, start_ref, total_ref, landed_ref, held_ref, sems):
    peers = plan_ref.shape[1]
    slot_total, rows, half = held_ref.shape
    locals_ = start_ref.shape[0]
    share = peers // PARTS

    def landing(part):
        piece = pl.ds(part * share, share)
        return pltpu.make_async_copy(second_ref.at[piece], landed_ref.at[piece], sems.at[part])

    def holding(group):
        piece = pl.ds(group * GROUP, GROUP)
        return pltpu.make_async_copy(
            tiles_ref.at[piece, :, pl.ds(half, half)], held_ref.at[piece], sems.at[PARTS + group]
        )

    for part in range(PARTS):
        landing(part).start()
    groups = slot_total // GROUP
    for group in range(groups):

        @pl.when(group <= slots_ref[LAST, 0])
        def _():
            holding(group).start()

    total_ref[pl.ds(0, locals_)] = start_ref[...]

    def add(q, carry):
        block = plan_ref[ASKED, q]

        @pl.when(block >= 0)
        def _():
            total_ref[block] += landed_ref[q, pl.ds(0, rows)].astype(jnp.float32)

        return carry

    for part in range(PARTS):
        landing(part).wait()
        lax.fori_loop(part * share, (part + 1) * share, add, 0, unroll=4)

    def multiply(group, carry):
        @pl.when(group <= slots_ref[LAST, 0])
        def _():
            holding(group).wait()
            for at in range(GROUP):
                slot = group * GROUP + at
                home = slots_ref[HOME, slot]
                remote = slots_ref[COLUMN, slot] == locals_
                row = jnp.where(remote, slots_ref[ROW, slot], locals_)
                via = plan_ref[CAME_VIA, home]
                source = jnp.where(via >= 0, via, home)
                offset = pl.multiple_of(jnp.where(via >= 0, half, 0), half)
                total_ref[row] += jnp.dot(
                    held_ref[slot],
                    landed_ref[source, pl.ds(offset, half)],
                    preferred_element_type=jnp.float32,
                )

        return carry

    lax.fori_loop(0, groups, multiply, 0)


def layer_kernel(
    plan_ref,
    slots_ref,
    second_ref,
    tiles_ref,
    start_ref,
    weight_ref,
    cotangent_ref,
    hidden_ref,
    upstream_ref,
    out_ref,
    total_ref,
    landed_ref,
    held_ref,
    late_sems,
    grad_ref,
    rows_ref,
    staged_ref,
    sems,
):
    late_sums(
        plan_ref,
        slots_ref,
        second_ref,
        tiles_ref,
        start_ref,
        total_ref,
        landed_ref,
        held_ref,
        late_sems,
    )
    peers = plan_ref.shape[1]
    half = held_ref.shape[2]
    width = upstream_ref.shape[2]
    weight = weight_ref[...]
    grad_ref[...] = jnp.zeros_like(grad_ref)

    def block_step(k, carry):
        aggregated = total_ref[k].astype(jnp.bfloat16)
        preact = jnp.dot(aggregated, weight, preferred_element_type=jnp.float32)
        sigma = 1.0 / (1.0 + jnp.exp(-preact))
        hidden_ref[k] = (preact * sigma).astype(jnp.bfloat16)
        delta = (
            cotangent_ref[k].astype(jnp.float32) * sigma * (1.0 + preact * (1.0 - sigma))
        ).astype(jnp.bfloat16)
        grad_ref[...] += lax.dot_general(
            aggregated, delta, (((0,), (0,)), ((), ())), preferred_element_type=jnp.float32
        )
        upstream_ref[k] = lax.dot_general(
            delta, weight, (((1,), (1,)), ((), ())), preferred_element_type=jnp.float32
        ).astype(jnp.bfloat16)
        return carry

    lax.fori_loop(0, cotangent_ref.shape[0], block_step, 0, unroll=2)
    for side in range(2):
        parts = three_parts(grad_ref[:, side * width : (side + 1) * width])
        for at, part in enumerate(parts):
            rows_ref[:, 2 * at + side, :] = part
    for at in range(6, EXTRA):
        rows_ref[:, at, :] = jnp.zeros((peers, width), jnp.float32)
    staged_ref[...] = rows_ref[...].astype(jnp.bfloat16)
    put = pltpu.make_async_copy(staged_ref, out_ref.at[:, pl.ds(half, EXTRA)], sems.at[2 * peers])
    put.start()
    send_first(plan_ref, upstream_ref, out_ref, sems)
    put.wait()


def layer(plan, slots, second, tile_values, start, weight, cotangent):
    peers, _, width = second.shape
    _, rows, _ = tile_values.shape
    locals_ = start.shape[0]
    hid = weight.shape[1]
    assert width == peers and hid == 2 * width
    anywhere = pl.BlockSpec(memory_space=pl.ANY)
    return pl.pallas_call(
        layer_kernel,
        grid_spec=pltpu.PrefetchScalarGridSpec(
            num_scalar_prefetch=2,
            grid=(1,),
            in_specs=[
                anywhere,
                anywhere,
                whole(*start.shape),
                whole(width, hid),
                whole(locals_, rows, hid),
            ],
            out_specs=[whole(locals_, rows, hid), whole(locals_, rows, width), anywhere],
            scratch_shapes=late_scratch(second, tile_values, start)
            + [
                pltpu.VMEM((width, hid), jnp.float32),
                pltpu.VMEM((peers, EXTRA, width), jnp.float32),
                pltpu.VMEM((peers, EXTRA, width), jnp.bfloat16),
                pltpu.SemaphoreType.DMA((2 * peers + 1,)),
            ],
        ),
        out_shape=[
            jax.ShapeDtypeStruct((locals_, rows, hid), jnp.bfloat16),
            jax.ShapeDtypeStruct((locals_, rows, width), jnp.bfloat16),
            jax.ShapeDtypeStruct((peers, rows // 2 + EXTRA, width), jnp.bfloat16),
        ],
        compiler_params=params(),
    )(plan, slots, second, tile_values, start, weight, cotangent)


def last_kernel(
    scale,
    plan_ref,
    slots_ref,
    second_ref,
    tiles_ref,
    start_ref,
    out_ref,
    weight_grad_ref,
    total_ref,
    landed_ref,
    held_ref,
    late_sems,
    rows_ref,
):
    late_sums(
        plan_ref,
        slots_ref,
        second_ref,
        tiles_ref,
        start_ref,
        total_ref,
        landed_ref,
        held_ref,
        late_sems,
    )
    rows = held_ref.shape[1]
    width = out_ref.shape[2]
    out_ref[...] = total_ref[pl.ds(0, out_ref.shape[0])].astype(out_ref.dtype)
    rows_ref[...] = landed_ref[:, pl.ds(rows, EXTRA)].astype(jnp.float32)
    for side in range(2):
        weight_grad_ref[:, side * width : (side + 1) * width] = (
            rows_ref[:, 4 + side, :] + rows_ref[:, 2 + side, :] + rows_ref[:, side, :]
        ) * scale


def last(plan, slots, second, tile_values, start, scale):
    peers, _, width = second.shape
    _, rows, _ = tile_values.shape
    locals_ = start.shape[0]
    anywhere = pl.BlockSpec(memory_space=pl.ANY)
    return pl.pallas_call(
        functools.partial(last_kernel, scale),
        grid_spec=pltpu.PrefetchScalarGridSpec(
            num_scalar_prefetch=2,
            grid=(1,),
            in_specs=[anywhere, anywhere, whole(*start.shape)],
            out_specs=[whole(locals_, rows, width), whole(peers, 2 * width)],
            scratch_shapes=late_scratch(second, tile_values, start)
            + [pltpu.VMEM((peers, EXTRA, width), jnp.float32)],
        ),
        out_shape=[
            jax.ShapeDtypeStruct((locals_, rows, width), jnp.bfloat16),
            jax.ShapeDtypeStruct((peers, 2 * width), jnp.float32),
        ],
        compiler_params=params(),
    )(plan, slots, second, tile_values, start)


def on_device(features, weight, cotangent, block_pairs, tile_counts, tile_values):
    peers = lax.axis_size("nodes")
    myself = lax.axis_index("nodes")
    rows = tile_values.shape[1]
    width = features.shape[1]
    hid = weight.shape[1]
    locals_ = features.shape[0] // rows
    count = tile_counts[0]
    slot_ids = jnp.arange(block_pairs.shape[0], dtype=jnp.int32)
    peer_ids = jnp.arange(peers, dtype=jnp.int32)
    row_local = jnp.clip(block_pairs[:, 0] - myself * locals_, 0, locals_ - 1)
    col_blocks = block_pairs[:, 1]
    home = col_blocks // locals_
    column = col_blocks % locals_
    live = slot_ids < count
    remote = live & (home != myself)
    hit = (home[None, :] == peer_ids[:, None]) & remote[None, :]
    wanted = jnp.max(jnp.where(hit, column[None, :], -1), axis=1)
    named_twice = jnp.sum(hit.astype(jnp.int32), axis=1) > 1
    wanted = wanted + jnp.where(named_twice, TWICE, 0)
    everyones = exchange(jnp.broadcast_to(wanted[None, :], (peers, peers)))
    plan = make_plan(myself, everyones)
    blocks = features.reshape(locals_, rows, width)
    cotangent_blocks = cotangent.reshape(locals_, rows, hid)
    scale = 1.0 / math.sqrt(peers * locals_ * rows)

    def sparse():
        slots = jnp.stack(
            [
                row_local,
                jnp.where(remote, home, myself),
                jnp.where(live & ~remote, column, jnp.where(remote, locals_, locals_ + 1)),
                jnp.broadcast_to((count - 1) // GROUP, row_local.shape),
            ]
        )
        first = exchange(first_halves(plan, blocks))
        outgoing, total = own_products(plan, slots, blocks, tile_values, 0)
        first, outgoing = lax.optimization_barrier((first, outgoing))
        second = exchange(relay(plan, first, outgoing, False))
        total = early_products(plan, slots, first, tile_values, total)
        hidden, upstream, sending = layer(
            plan, slots, second, tile_values, total, weight, cotangent_blocks
        )
        first = exchange(sending)
        outgoing, total = own_products(plan, slots, upstream, tile_values, EXTRA)
        first, outgoing = lax.optimization_barrier((first, outgoing))
        second = exchange(relay(plan, first, outgoing, True))
        total = early_products(plan, slots, first, tile_values, total)
        feature_grad, weight_grad = last(plan, slots, second, tile_values, total, scale)
        return hidden, weight_grad, feature_grad

    def full():
        asked = plan[ASKED]
        asked = jnp.where(asked >= 0, asked % TWICE, -1)
        dest = jnp.where(live, jnp.where(remote, home, peers + column), -1)
        earlier = (home[None, :] == home[:, None]) & (slot_ids[None, :] < slot_ids[:, None])
        again = jnp.any(earlier, axis=1).astype(jnp.int32)
        arrived = exchange(pick(asked, blocks))
        outgoing, total = transposed_products(row_local, dest, again, blocks, tile_values, peers)
        returned = exchange(outgoing)
        total = direct_products(row_local, dest, arrived, tile_values, total)
        hidden, local_grad, upstream, sending = dense(
            asked, returned, total, weight, cotangent_blocks
        )
        weight_grad = lax.psum(local_grad, "nodes") * scale
        arrived = exchange(sending)
        outgoing, total = transposed_products(row_local, dest, again, upstream, tile_values, peers)
        returned = exchange(outgoing)
        total = direct_products(row_local, dest, arrived, tile_values, total)
        return hidden, weight_grad, finish(asked, returned, total)

    hidden, weight_grad, feature_grad = lax.cond(plan[FITS, 0] > 0, sparse, full)
    return (
        hidden.reshape(locals_ * rows, hid),
        weight_grad,
        feature_grad.reshape(locals_ * rows, width),
    )


def solution(mesh):
    return jax.shard_map(
        on_device,
        mesh=mesh,
        in_specs=(
            P("nodes", None),
            P(),
            P("nodes", None),
            P("nodes", None),
            P("nodes"),
            P("nodes", None, None),
        ),
        out_specs=(P("nodes", None), P(), P("nodes", None)),
        check_vma=False,
    )
```

time: 814 us -> 452 us (0.56); the launches traced: 803 us -> 451 us
  local copies, waits for them, and re-layouts: 165 us -> 1.9 us
  waiting for transfers between devices: 422 us -> 264 us
  Pallas kernels: 0 us -> 120 us
  matrix products: 101 us -> 0 us
  other arithmetic: 52.4 us -> 2.86 us
    psum x1 -> x0, waiting for transfers between devices: 207 us -> none  [on_device(): lax.psum(local_grad, 'nodes') / jnp.sqrt(jnp.float32(node_total))]
    pallas_call x0 -> x10, Pallas kernels: none -> 120 us  [the longest x2 50.1 us: own_products(): pl.pallas_call(products_kernel, grid_spec=pltpu.PrefetchScalarGridSpec(nu...]
    dot_general x13 -> x0, matrix products: 101 us -> none  [the longest x2 32 us: aggregate(): jnp.einsum('jab,jbf->jaf', tile_values, fetched, preferred_element_type=j...]
    gather x10 -> x0, local copies, waits for them, and re-layouts: 87.2 us -> none  [the longest x4 36.7 us: aggregate(): jnp.take(blocks, jnp.maximum(asked, 0), axis=0)]
    dot_general x4 -> x0, local copies, waits for them, and re-layouts: 50.7 us -> none  [the longest x2 25.4 us: aggregate(): jnp.einsum('jab,jaf->jbf', tile_values, own_rows, preferred_element_type=...]
    all_to_all x5, waiting for transfers between devices: 215 us -> 264 us  [exchange(): lax.all_to_all(values, 'nodes', split_axis=0, concat_axis=0, tiled=True)]
    select_n x5 -> x1, other arithmetic: 30.3 us -> 0.69 us  [on_device(): column = col_blocks % locals_]
    all_to_all x3 -> x0, local copies, waits for them, and re-layouts: 25.5 us -> none  [the longest x2 24.8 us: aggregate(): lax.all_to_all(outgoing, 'nodes', split_axis=0, concat_axis=0, tiled=True)]
  transfers between devices with their start and end apart: 6 -> 5, of which waited for: 4 -> 5; matrix products, arithmetic and copies ran while one was open for 26% -> 0% of each run, Pallas kernels for 0% -> 15%
where the time goes in v1:
time: 452 us; the launch traced here: 451 us
  waiting for transfers between devices  264 us (58%)
  Pallas kernels  120 us (27%)
  starting transfers between devices  45.6 us (10%)
  between operations  15.4 us (3%)
    all_to_all x5, waiting for transfers between devices, exchange(): lax.all_to_all(values, 'nodes', split_axis=0, concat_axis=0, tiled=True)  264 us
    pallas_call x2, Pallas kernels, own_products(): pl.pallas_call(products_kernel, grid_spec=pltpu.PrefetchScalarGridSpec(nu...  50.1 us
    all_to_all x5, starting transfers between devices, exchange(): lax.all_to_all(values, 'nodes', split_axis=0, concat_axis=0, tiled=True)  45.6 us
    pallas_call x1, Pallas kernels, layer(): pl.pallas_call(layer_kernel, grid_spec=pltpu.PrefetchScalarGridSpec(num_s...  17.2 us
    pallas_call x2, Pallas kernels, early_products(): pl.pallas_call(early_kernel, grid_spec=pltpu.PrefetchScalarGridSpec(num_s...  15.3 us
    pallas_call x2, Pallas kernels, relay(): pl.pallas_call(relay_kernel, grid_spec=pltpu.PrefetchScalarGridSpec(num_s...  11.6 us
    pallas_call x1, Pallas kernels, make_plan(): pl.pallas_call(plan_kernel, grid_spec=pltpu.PrefetchScalarGridSpec(num_sc...  10.1 us
    pallas_call x1, Pallas kernels, last(): pl.pallas_call(functools.partial(last_kernel, scale), grid_spec=pltpu.Pre...  9.05 us
  transfers between devices with their start and end apart: 5, of which 5 were waited for; matrix products, arithmetic and copies ran while one was open for 0% of the time, Pallas kernels for 15%

profile of v1, /device:TPU:38, one launch (start us, length us, event | category | flops | bytes accessed | tf_op | source)
XLA Modules:
  0.0 450.9 jit_solution(8125681560107580956)
XLA Ops:
  7.8 0.7 and_select_fusion.2
  8.5 0.7 compare_and_fusion
  10.0 10.2 %all-to-all-start.8 = ((s32[128,1,128]{2,1,0:T(1,128)}), s32[128,1,128]{2,1,0:T(1,128)S(1)}, u32[]{:S(2)}, u32[]{:S(2)}) async-start(s32[128,1,128]{2,1,0:T(1,128)} %broadcast_in_dim.65), calls=%async_computation.8 | async-start | bytes 131072 | tf_op jit(solution)/shard_map/all_to_all | solution.py:312
  20.2 0.7 clamp_bitcast_fusion
  20.9 6.2 %all-to-all-done.8 = s32[128,1,128]{2,1,0:T(1,128)S(1)} async-done(((s32[128,1,128]{2,1,0:T(1,128)}), s32[128,1,128]{2,1,0:T(1,128)S(1)}, u32[]{:S(2)}, u32[]{:S(2)}) %all-to-all-start.8) | async-done | bytes 65568 | tf_op jit(solution)/shard_map/all_to_all | solution.py:312
  27.8 10.1 %shard_map.85 = s32[8,128]{1,0:T(8,128)S(1)} custom-call(s32[1]{0:T(128)} %bitcast.6.me_ref, s32[128,128]{1,0:T(8,128)} %bitcast.40), custom_call_target="tpu_custom_call" | custom-call | tf_op jit(solution)/shard_map/pallas_call | solution.py:375
  39.0 405.0 %conditional.1 = (bf16[8,256,256]{2,1,0:T(8,128)(2,1)}, f32[128,256]{1,0:T(8,128)}, bf16[2048,128]{1,0:T(8,128)(2,1)}) conditional(s32[]{:T(128)} %bitcast.10, (s32[8,128]{1,0:T(8,128)S(1)}, s32[96]{0:T(128)S(1)}, pred[96]{0:T(512)(128)(4,1)S(1)}, s32[96]{0:T(128)S(1)}, pred[96]{0:T(512)(128)(4,1)S(1)}, /*index=5*/s32[96]{0:T(128)S(1)}, ...), branch_computations={%region_2.5_spmd, %region_5.6_spmd} | conditional | flops 8053168128 | bytes 208932768 | solution.py:972
  39.1 6.5 %branch_1_fun.9 = bf16[128,128,128]{2,1,0:T(8,128)(2,1)} custom-call(s32[8,128]{1,0:T(8,128)S(1)} %get-tuple-element.66.plan_ref, bf16[8,256,128]{2,1,0:T(8,128)(2,1)} %get-tuple-element.74.blocks_ref), custom_call_target="tpu_custom_call" | custom-call | tf_op jit(solution)/shard_map/cond/branch_1_fun/pallas_call | solution.py:441
  45.6 8.4 %all-to-all-start.4 = ((bf16[128,128,128]{2,1,0:T(8,128)(2,1)}), bf16[128,128,128]{2,1,0:T(8,128)(2,1)}, u32[]{:S(2)}, u32[]{:S(2)}) async-start(bf16[128,128,128]{2,1,0:T(8,128)(2,1)} %branch_1_fun.9), calls=%async_computation.4 | async-start | bytes 8388608 | tf_op jit(solution)/shard_map/cond/branch_1_fun/all_to_all | solution.py:312
  55.4 25.0 %branch_1_fun.10 = (bf16[128,256,128]{2,1,0:T(8,128)(2,1)}, f32[8,256,128]{2,1,0:T(8,128)}) custom-call(s32[8,128]{1,0:T(8,128)S(1)} %get-tuple-element.66.plan_ref, s32[4,96]{1,0:T(4,128)} %add_add_fusion.slots_ref, bf16[8,256,128]{2,1,0:T(8,128)(2,1)S(1)} %copy-done.1, bf16[96,256,256]{2,1,0:T(8,128)(2,1)} %get-tuple-element.75.tiles_ref), custom_call_target="tpu_custom_call" | custom-call | flops 2415919104 | bytes 25165824 | tf_op jit(solution)/shard_map/cond/branch_1_fun/pallas_call | solution.py:505
  80.4 23.9 %all-to-all-done.4.came_ref.first_ref = bf16[128,128,128]{2,1,0:T(8,128)(2,1)} async-done(((bf16[128,128,128]{2,1,0:T(8,128)(2,1)}), bf16[128,128,128]{2,1,0:T(8,128)(2,1)}, u32[]{:S(2)}, u32[]{:S(2)}) %all-to-all-start.4) | async-done | bytes 4194336 | tf_op jit(solution)/shard_map/cond/branch_1_fun/all_to_all | solution.py:312
  104.3 5.6 %branch_1_fun.11 = bf16[128,256,128]{2,1,0:T(8,128)(2,1)} custom-call(s32[8,128]{1,0:T(8,128)S(1)} %get-tuple-element.66.plan_ref, bf16[128,128,128]{2,1,0:T(8,128)(2,1)} %all-to-all-done.4.came_ref.first_ref, bf16[128,256,128]{2,1,0:T(8,128)(2,1)} %get-tuple-element.78._), custom_call_target="tpu_custom_call", output_to_operand_aliasing={{}: (2, {})} | custom-call | tf_op jit(solution)/shard_map/cond/branch_1_fun/pallas_call | solution.py:596
  109.9 8.4 %all-to-all-start.5 = ((bf16[128,256,128]{2,1,0:T(8,128)(2,1)}), bf16[128,256,128]{2,1,0:T(8,128)(2,1)}, u32[]{:S(2)}, u32[]{:S(2)}) async-start(bf16[128,256,128]{2,1,0:T(8,128)(2,1)} %branch_1_fun.11), calls=%async_computation.5 | async-start | bytes 16777216 | tf_op jit(solution)/shard_map/cond/branch_1_fun/all_to_all | solution.py:312
  118.3 7.6 %branch_1_fun.12.start_ref = f32[8,256,128]{2,1,0:T(8,128)} custom-call(s32[8,128]{1,0:T(8,128)S(1)} %get-tuple-element.66.plan_ref, s32[4,96]{1,0:T(4,128)} %add_add_fusion.slots_ref, bf16[128,128,128]{2,1,0:T(8,128)(2,1)} %all-to-all-done.4.came_ref.first_ref, bf16[96,256,256]{2,1,0:T(8,128)(2,1)} %get-tuple-element.75.tiles_ref, ...), custom_call_target="tpu_custom_call" | custom-call | flops 805306368 | bytes 12582912 | tf_op jit(solution)/shard_map/cond/branch_1_fun/pallas_call | solution.py:640
  125.9 96.1 %all-to-all-done.5.second_ref = bf16[128,256,128]{2,1,0:T(8,128)(2,1)} async-done(((bf16[128,256,128]{2,1,0:T(8,128)(2,1)}), bf16[128,256,128]{2,1,0:T(8,128)(2,1)}, u32[]{:S(2)}, u32[]{:S(2)}) %all-to-all-start.5) | async-done | bytes 8388640 | tf_op jit(solution)/shard_map/cond/branch_1_fun/all_to_all | solution.py:312
  222.1 17.2 %branch_1_fun.13 = (bf16[8,256,256]{2,1,0:T(8,128)(2,1)}, bf16[8,256,128]{2,1,0:T(8,128)(2,1)}, bf16[128,144,128]{2,1,0:T(8,128)(2,1)}) custom-call(s32[8,128]{1,0:T(8,128)S(1)} %get-tuple-element.66.plan_ref, s32[4,96]{1,0:T(4,128)} %add_add_fusion.slots_ref, bf16[128,256,128]{2,1,0:T(8,128)(2,1)} %all-to-all-done.5.second_ref, ...), custom_call_target="tpu_custom_call" | custom-call | tf_op jit(solution)/shard_map/cond/branch_1_fun/pallas_call | solution.py:812
  239.3 9.9 %all-to-all-start.6 = ((bf16[128,144,128]{2,1,0:T(8,128)(2,1)}), bf16[128,144,128]{2,1,0:T(8,128)(2,1)}, u32[]{:S(2)}, u32[]{:S(2)}) async-start(bf16[128,144,128]{2,1,0:T(8,128)(2,1)} %get-tuple-element.83), calls=%async_computation.6 | async-start | bytes 9437184 | tf_op jit(solution)/shard_map/cond/branch_1_fun/all_to_all | solution.py:312
  249.1 25.1 %branch_1_fun.14 = (bf16[128,272,128]{2,1,0:T(8,128)(2,1)}, f32[8,256,128]{2,1,0:T(8,128)}) custom-call(s32[8,128]{1,0:T(8,128)S(1)} %get-tuple-element.66.plan_ref, s32[4,96]{1,0:T(4,128)} %add_add_fusion.slots_ref, bf16[8,256,128]{2,1,0:T(8,128)(2,1)} %get-tuple-element.84.blocks_ref, bf16[96,256,256]{2,1,0:T(8,128)(2,1)} %get-tuple-element.75.tiles_ref), custom_call_target="tpu_custom_call" | custom-call | flops 2415919104 | bytes 25165824 | tf_op jit(solution)/shard_map/cond/branch_1_fun/pallas_call | solution.py:505
  274.3 31.1 %all-to-all-done.6.came_ref.first_ref = bf16[128,144,128]{2,1,0:T(8,128)(2,1)} async-done(((bf16[128,144,128]{2,1,0:T(8,128)(2,1)}), bf16[128,144,128]{2,1,0:T(8,128)(2,1)}, u32[]{:S(2)}, u32[]{:S(2)}) %all-to-all-start.6) | async-done | bytes 4718624 | tf_op jit(solution)/shard_map/cond/branch_1_fun/all_to_all | solution.py:312
  305.4 6.0 %branch_1_fun.15 = bf16[128,272,128]{2,1,0:T(8,128)(2,1)} custom-call(s32[8,128]{1,0:T(8,128)S(1)} %get-tuple-element.66.plan_ref, bf16[128,144,128]{2,1,0:T(8,128)(2,1)} %all-to-all-done.6.came_ref.first_ref, bf16[128,272,128]{2,1,0:T(8,128)(2,1)} %get-tuple-element.87._), custom_call_target="tpu_custom_call", output_to_operand_aliasing={{}: (2, {})} | custom-call | tf_op jit(solution)/shard_map/cond/branch_1_fun/pallas_call | solution.py:596
  311.4 8.7 %all-to-all-start.7 = ((bf16[128,272,128]{2,1,0:T(8,128)(2,1)}), bf16[128,272,128]{2,1,0:T(8,128)(2,1)}, u32[]{:S(2)}, u32[]{:S(2)}) async-start(bf16[128,272,128]{2,1,0:T(8,128)(2,1)} %branch_1_fun.15), calls=%async_computation.7 | async-start | bytes 17825792 | tf_op jit(solution)/shard_map/cond/branch_1_fun/all_to_all | solution.py:312
  320.1 7.7 %branch_1_fun.16.start_ref = f32[8,256,128]{2,1,0:T(8,128)} custom-call(s32[8,128]{1,0:T(8,128)S(1)} %get-tuple-element.66.plan_ref, s32[4,96]{1,0:T(4,128)} %add_add_fusion.slots_ref, bf16[128,144,128]{2,1,0:T(8,128)(2,1)} %all-to-all-done.6.came_ref.first_ref, bf16[96,256,256]{2,1,0:T(8,128)(2,1)} %get-tuple-element.75.tiles_ref, ...), custom_call_target="tpu_custom_call" | custom-call | flops 805306368 | bytes 12582912 | tf_op jit(solution)/shard_map/cond/branch_1_fun/pallas_call | solution.py:640
  327.8 107.0 %all-to-all-done.7.second_ref = bf16[128,272,128]{2,1,0:T(8,128)(2,1)} async-done(((bf16[128,272,128]{2,1,0:T(8,128)(2,1)}), bf16[128,272,128]{2,1,0:T(8,128)(2,1)}, u32[]{:S(2)}, u32[]{:S(2)}) %all-to-all-start.7) | async-done | bytes 8912928 | tf_op jit(solution)/shard_map/cond/branch_1_fun/all_to_all | solution.py:312
  434.8 9.0 %branch_1_fun.17 = (bf16[8,256,128]{2,1,0:T(8,128)(2,1)}, f32[128,256]{1,0:T(8,128)}) custom-call(s32[8,128]{1,0:T(8,128)S(1)} %get-tuple-element.66.plan_ref, s32[4,96]{1,0:T(4,128)} %add_add_fusion.slots_ref, bf16[128,272,128]{2,1,0:T(8,128)(2,1)} %all-to-all-done.7.second_ref, bf16[96,256,256]{2,1,0:T(8,128)(2,1)} %get-tuple-element.75.tiles_ref, ...), custom_call_target="tpu_custom_call" | custom-call | tf_op jit(solution)/shard_map/cond/branch_1_fun/pallas_call | solution.py:883
  (17 shorter events, 2.7 us)
Async XLA Ops:
  10.0 17.1 %all-to-all-start.8 = ((s32[128,1,128]{2,1,0:T(1,128)}), s32[128,1,128]{2,1,0:T(1,128)S(1)}, u32[]{:S(2)}, u32[]{:S(2)}) async-start(s32[128,1,128]{2,1,0:T(1,128)} %broadcast_in_dim.65), calls=%async_computation.8 | async-start | bytes 131072 | tf_op jit(solution)/shard_map/all_to_all | solution.py:312
  27.1 0.6 copy-start.6
  39.1 16.3 %copy-start.1 = (bf16[8,256,128]{2,1,0:T(8,128)(2,1)S(1)}, bf16[8,256,128]{2,1,0:T(8,128)(2,1)}, u32[]{:S(2)}) copy-start(bf16[8,256,128]{2,1,0:T(8,128)(2,1)} %get-tuple-element.74.blocks_ref) | copy-start | bytes 1572868 | tf_op jit(solution)/shard_map/cond
  45.6 58.7 %all-to-all-start.4 = ((bf16[128,128,128]{2,1,0:T(8,128)(2,1)}), bf16[128,128,128]{2,1,0:T(8,128)(2,1)}, u32[]{:S(2)}, u32[]{:S(2)}) async-start(bf16[128,128,128]{2,1,0:T(8,128)(2,1)} %branch_1_fun.9), calls=%async_computation.4 | async-start | bytes 8388608 | tf_op jit(solution)/shard_map/cond/branch_1_fun/all_to_all | solution.py:312
  109.9 112.2 %all-to-all-start.5 = ((bf16[128,256,128]{2,1,0:T(8,128)(2,1)}), bf16[128,256,128]{2,1,0:T(8,128)(2,1)}, u32[]{:S(2)}, u32[]{:S(2)}) async-start(bf16[128,256,128]{2,1,0:T(8,128)(2,1)} %branch_1_fun.11), calls=%async_computation.5 | async-start | bytes 16777216 | tf_op jit(solution)/shard_map/cond/branch_1_fun/all_to_all | solution.py:312
  118.3 103.8 %copy-start.3 = (bf16[8,256,256]{2,1,0:T(8,128)(2,1)S(1)}, bf16[8,256,256]{2,1,0:T(8,128)(2,1)}, u32[]{:S(2)}) copy-start(bf16[8,256,256]{2,1,0:T(8,128)(2,1)} %get-tuple-element.81.cotangent_ref) | copy-start | bytes 3145732 | tf_op jit(solution)/shard_map/cond
  118.3 103.8 %copy-start.5 = (bf16[128,256]{1,0:T(8,128)(2,1)S(1)}, bf16[128,256]{1,0:T(8,128)(2,1)}, u32[]{:S(2)}) copy-start(bf16[128,256]{1,0:T(8,128)(2,1)} %get-tuple-element.80.weight_ref) | copy-start | bytes 196612 | tf_op jit(solution)/shard_map/cond
  239.3 66.1 %all-to-all-start.6 = ((bf16[128,144,128]{2,1,0:T(8,128)(2,1)}), bf16[128,144,128]{2,1,0:T(8,128)(2,1)}, u32[]{:S(2)}, u32[]{:S(2)}) async-start(bf16[128,144,128]{2,1,0:T(8,128)(2,1)} %get-tuple-element.83), calls=%async_computation.6 | async-start | bytes 9437184 | tf_op jit(solution)/shard_map/cond/branch_1_fun/all_to_all | solution.py:312
  311.4 123.4 %all-to-all-start.7 = ((bf16[128,272,128]{2,1,0:T(8,128)(2,1)}), bf16[128,272,128]{2,1,0:T(8,128)(2,1)}, u32[]{:S(2)}, u32[]{:S(2)}) async-start(bf16[128,272,128]{2,1,0:T(8,128)(2,1)} %branch_1_fun.15), calls=%async_computation.7 | async-start | bytes 17825792 | tf_op jit(solution)/shard_map/cond/branch_1_fun/all_to_all | solution.py:312

commit v2 on v1

--- a/solution.py
+++ b/solution.py
@@ -13,6 +13,7 @@
 PARTS = 4
 EXTRA = 16
 TWICE = 64
+TURNS = 8
 
 
 def whole(*shape):
@@ -316,44 +317,65 @@
 OPEN = -2
 
 
-def plan_kernel(me_ref, wanted_ref, plan_ref, free_ref, rows_ref, columns_ref):
+def plan_kernel(
+    me_ref, wanted_ref, blocks_ref, plan_ref, out_ref, free_ref, rows_ref, columns_ref, known_ref, sems
+):
     peers = wanted_ref.shape[0]
+    groups = peers // 8
     me = me_ref[0]
     raw = wanted_ref[...]
     u_ids = lax.broadcasted_iota(jnp.int32, raw.shape, 0)
-    v_ids = lax.broadcasted_iota(jnp.int32, raw.shape, 1)
     named = (raw >= 0).astype(jnp.float32)
     flipped = named.T
     skewed = flipped
     for bit in range(peers.bit_length() - 1):
         turned = pltpu.roll(skewed, peers - (1 << bit), 1)
         skewed = jnp.where(((u_ids >> bit) & 1) == 1, turned, skewed)
-    free_ref[...] = (1.0 - skewed.T).astype(jnp.int32)
+    free = (1.0 - skewed.T).astype(jnp.int32)
+    free_ref[...] = jnp.broadcast_to(free[:, None, :], free_ref.shape)
     route = jnp.where((named > 0) & (flipped > 0), OPEN, -1)
     spare = 1 - flipped.astype(jnp.int32)
-
-    def left_open(route):
-        return jnp.sum((route == OPEN).astype(jnp.float32)).astype(jnp.int32)
-
-    def one(turn, carry):
-        route, spare = carry
-        fits = (route == OPEN) & ((spare & free_ref[pl.ds(turn, 1), :]) > 0)
-        first = jnp.min(jnp.where(fits, u_ids, peers), axis=0, keepdims=True)
-        chosen = fits & (u_ids == first)
-        route = jnp.where(chosen, (v_ids + turn) & (peers - 1), route)
-        spare = jnp.where(chosen, 0, spare)
-        return route, pltpu.roll(spare, peers - 1, 1)
+    at_ids = lax.broadcasted_iota(jnp.int32, (8, peers), 0)
+    v_ids = lax.broadcasted_iota(jnp.int32, (8, peers), 1)
+
+    def left_open(routes):
+        count = (routes[0] == OPEN).astype(jnp.float32)
+        for part in routes[1:]:
+            count += (part == OPEN).astype(jnp.float32)
+        return jnp.sum(count).astype(jnp.int32)
+
+    def one(turn, routes, spares):
+        shifts = [(turn + 8 * group) & (peers - 1) for group in range(groups)]
+        rooms = [free_ref[shift] for shift in shifts]
+        next_routes, next_spares, taken = [], [], []
+        for route, spare, shift, room in zip(routes, spares, shifts, rooms):
+            fits = (route == OPEN) & ((spare & room) > 0)
+            first = jnp.min(jnp.where(fits, at_ids, 8), axis=0, keepdims=True)
+            chosen = fits & (at_ids == first)
+            taken.append(jnp.where(first < 8, 0, room))
+            next_routes.append(jnp.where(chosen, (v_ids + shift) & (peers - 1), route))
+            next_spares.append(pltpu.roll(jnp.where(chosen, 0, spare), peers - 1, 1))
+        for shift, room in zip(shifts, taken):
+            free_ref[shift] = room
+        return tuple(next_routes), tuple(next_spares)
 
     def some(carry):
-        turn, _, route, spare = carry
-        route, spare = lax.fori_loop(0, 8, lambda i, c: one(turn + i, c), (route, spare))
-        return turn + 8, left_open(route), route, spare
-
-    _, left, route, _ = lax.while_loop(
+        turn, _, routes, spares = carry
+        for ahead in range(TURNS):
+            routes, spares = one(turn + ahead, routes, spares)
+        return turn + TURNS, left_open(routes), routes, spares
+
+    routes = tuple(route[8 * group : 8 * group + 8] for group in range(groups))
+    spares = tuple(
+        pltpu.roll(spare[8 * group : 8 * group + 8], (peers - 8 * group) % peers, 1)
+        for group in range(groups)
+    )
+    _, left, routes, _ = lax.while_loop(
         lambda carry: (carry[0] < peers) & (carry[1] > 0),
         some,
-        (jnp.int32(0), left_open(route), route, spare),
+        (jnp.int32(0), left_open(routes), routes, spares),
     )
+    route = jnp.concatenate(routes, 0)
     rows_ref[...] = route
     columns_ref[...] = route.astype(jnp.float32).T.astype(jnp.int32)
     plan_ref[VIA : VIA + 1, :] = rows_ref[pl.ds(me, 1), :]
@@ -367,23 +389,40 @@
     twice = jnp.sum((raw >= TWICE).astype(jnp.float32)).astype(jnp.int32)
     fits = jnp.where((left == 0) & (twice == 0), 1, 0)
     plan_ref[FITS:, :] = jnp.full((plan_ref.shape[0] - FITS, peers), fits, jnp.int32)
-
-
-def make_plan(myself, wanted):
+    tell = pltpu.make_async_copy(plan_ref, known_ref, sems.at[2 * peers])
+    tell.start()
+    tell.wait()
+
+    @pl.when(fits > 0)
+    def _():
+        send_first(known_ref, blocks_ref, out_ref, sems)
+
+
+def make_plan(myself, wanted, blocks):
     peers = wanted.shape[0]
+    locals_, rows, width = blocks.shape
     square = pltpu.VMEM((peers, peers), jnp.int32)
     return pl.pallas_call(
         plan_kernel,
         grid_spec=pltpu.PrefetchScalarGridSpec(
             num_scalar_prefetch=1,
             grid=(1,),
-            in_specs=[whole(peers, peers)],
-            out_specs=whole(8, peers),
-            scratch_shapes=[square, square, square],
-        ),
-        out_shape=jax.ShapeDtypeStruct((8, peers), jnp.int32),
+            in_specs=[whole(peers, peers), whole(locals_, rows, width)],
+            out_specs=[whole(8, peers), pl.BlockSpec(memory_space=pl.ANY)],
+            scratch_shapes=[
+                pltpu.VMEM((peers, 8, peers), jnp.int32),
+                square,
+                square,
+                pltpu.SMEM((8, peers), jnp.int32),
+                pltpu.SemaphoreType.DMA((2 * peers + 1,)),
+            ],
+        ),
+        out_shape=[
+            jax.ShapeDtypeStruct((8, peers), jnp.int32),
+            jax.ShapeDtypeStruct((peers, rows // 2, width), blocks.dtype),
+        ],
         compiler_params=params(),
-    )(jnp.full((1,), myself, jnp.int32), wanted)
+    )(jnp.full((1,), myself, jnp.int32), wanted, blocks)
 
 
 def each_peer(peers, act):
@@ -433,23 +472,6 @@
 
     each_peer(peers, start)
     each_peer(peers, wait)
-
-
-def first_halves(plan, blocks):
-    peers = plan.shape[1]
-    locals_, rows, width = blocks.shape
-    return pl.pallas_call(
-        send_first,
-        grid_spec=pltpu.PrefetchScalarGridSpec(
-            num_scalar_prefetch=1,
-            grid=(1,),
-            in_specs=[whole(locals_, rows, width)],
-            out_specs=pl.BlockSpec(memory_space=pl.ANY),
-            scratch_shapes=[pltpu.SemaphoreType.DMA((2 * peers,))],
-        ),
-        out_shape=jax.ShapeDtypeStruct((peers, rows // 2, width), blocks.dtype),
-        compiler_params=params(),
-    )(plan, blocks)
 
 
 def tiles_spec(rows):
@@ -919,8 +941,8 @@
     named_twice = jnp.sum(hit.astype(jnp.int32), axis=1) > 1
     wanted = wanted + jnp.where(named_twice, TWICE, 0)
     everyones = exchange(jnp.broadcast_to(wanted[None, :], (peers, peers)))
-    plan = make_plan(myself, everyones)
     blocks = features.reshape(locals_, rows, width)
+    plan, sending = make_plan(myself, everyones, blocks)
     cotangent_blocks = cotangent.reshape(locals_, rows, hid)
     scale = 1.0 / math.sqrt(peers * locals_ * rows)
 
@@ -933,15 +955,15 @@
                 jnp.broadcast_to((count - 1) // GROUP, row_local.shape),
             ]
         )
-        first = exchange(first_halves(plan, blocks))
+        first = exchange(sending)
         outgoing, total = own_products(plan, slots, blocks, tile_values, 0)
         first, outgoing = lax.optimization_barrier((first, outgoing))
         second = exchange(relay(plan, first, outgoing, False))
         total = early_products(plan, slots, first, tile_values, total)
-        hidden, upstream, sending = layer(
+        hidden, upstream, halves = layer(
             plan, slots, second, tile_values, total, weight, cotangent_blocks
         )
-        first = exchange(sending)
+        first = exchange(halves)
         outgoing, total = own_products(plan, slots, upstream, tile_values, EXTRA)
         first, outgoing = lax.optimization_barrier((first, outgoing))
         second = exchange(relay(plan, first, outgoing, True))
@@ -959,11 +981,12 @@
         outgoing, total = transposed_products(row_local, dest, again, blocks, tile_values, peers)
         returned = exchange(outgoing)
         total = direct_products(row_local, dest, arrived, tile_values, total)
-        hidden, local_grad, upstream, sending = dense(
+        hidden, local_grad, upstream, requested = dense(
             asked, returned, total, weight, cotangent_blocks
         )
-        weight_grad = lax.psum(local_grad, "nodes") * scale
-        arrived = exchange(sending)
+        row_sum = jnp.sum(exchange(local_grad), axis=0) * scale
+        weight_grad = exchange(jnp.broadcast_to(row_sum, local_grad.shape))
+        arrived = exchange(requested)
         outgoing, total = transposed_products(row_local, dest, again, upstream, tile_values, peers)
         returned = exchange(outgoing)
         total = direct_products(row_local, dest, arrived, tile_values, total)

time: 452 us -> 434 us (0.960)
  between operations: 15.4 us -> 2.16 us
    pallas_call x1 -> x0, Pallas kernels: 6.52 us -> none  [first_halves(): pl.pallas_call(send_first, grid_spec=pltpu.PrefetchScalarGridSpec(num_sca...]
where the time goes in v2:
time: 434 us; the launch traced here: 433 us
  waiting for transfers between devices  265 us (61%)
  Pallas kernels  116 us (27%)
  starting transfers between devices  44.2 us (10%)
    all_to_all x5, waiting for transfers between devices, exchange(): lax.all_to_all(values, 'nodes', split_axis=0, concat_axis=0, tiled=True)  265 us
    pallas_call x2, Pallas kernels, own_products(): pl.pallas_call(products_kernel, grid_spec=pltpu.PrefetchScalarGridSpec(nu...  50.4 us
    all_to_all x5, starting transfers between devices, exchange(): lax.all_to_all(values, 'nodes', split_axis=0, concat_axis=0, tiled=True)  44.2 us
    pallas_call x1, Pallas kernels, layer(): pl.pallas_call(layer_kernel, grid_spec=pltpu.PrefetchScalarGridSpec(num_s...  17.2 us
    pallas_call x2, Pallas kernels, early_products(): pl.pallas_call(early_kernel, grid_spec=pltpu.PrefetchScalarGridSpec(num_s...  15.3 us
    pallas_call x1, Pallas kernels, make_plan(): pl.pallas_call(plan_kernel, grid_spec=pltpu.PrefetchScalarGridSpec(num_sc...  12.3 us
    pallas_call x2, Pallas kernels, relay(): pl.pallas_call(relay_kernel, grid_spec=pltpu.PrefetchScalarGridSpec(num_s...  11.6 us
    pallas_call x1, Pallas kernels, last(): pl.pallas_call(functools.partial(last_kernel, scale), grid_spec=pltpu.Pre...  9.05 us
  transfers between devices with their start and end apart: 5, of which 5 were waited for; matrix products, arithmetic and copies ran while one was open for 0% of the time, Pallas kernels for 15%

profile of v2, /device:TPU:38, one launch (start us, length us, event | category | flops | bytes accessed | tf_op | source)
XLA Modules:
  0.0 433.1 jit_solution(14278377209037088087)
XLA Ops:
  1.3 0.7 and_select_fusion.2
  2.0 0.7 compare_and_fusion
  2.8 0.7 broadcast_in_dim.68
  3.5 10.2 %all-to-all-start.10 = ((s32[128,1,128]{2,1,0:T(1,128)}), s32[128,1,128]{2,1,0:T(1,128)S(1)}, u32[]{:S(2)}, u32[]{:S(2)}) async-start(s32[128,1,128]{2,1,0:T(1,128)} %broadcast_in_dim.68), calls=%async_computation.10 | async-start | bytes 131072 | tf_op jit(solution)/shard_map/all_to_all | solution.py:313
  13.7 0.7 clamp_bitcast_fusion
  14.4 6.3 %all-to-all-done.10 = s32[128,1,128]{2,1,0:T(1,128)S(1)} async-done(((s32[128,1,128]{2,1,0:T(1,128)}), s32[128,1,128]{2,1,0:T(1,128)S(1)}, u32[]{:S(2)}, u32[]{:S(2)}) %all-to-all-start.10) | async-done | bytes 65568 | tf_op jit(solution)/shard_map/all_to_all | solution.py:313
  21.2 12.3 %shard_map.85 = (s32[8,128]{1,0:T(8,128)S(1)}, bf16[128,128,128]{2,1,0:T(8,128)(2,1)}) custom-call(s32[1]{0:T(128)} %bitcast.7.me_ref, s32[128,128]{1,0:T(8,128)} %bitcast.44, bf16[8,256,128]{2,1,0:T(8,128)(2,1)} %bitcast.37), custom_call_target="tpu_custom_call" | custom-call | tf_op jit(solution)/shard_map/pallas_call | solution.py:405
  34.7 398.2 %conditional.1 = (bf16[8,256,256]{2,1,0:T(8,128)(2,1)}, f32[128,256]{1,0:T(8,128)}, bf16[2048,128]{1,0:T(8,128)(2,1)}) conditional(s32[]{:T(128)} %bitcast.12, (s32[8,128]{1,0:T(8,128)S(1)}, s32[96]{0:T(128)S(1)}, pred[96]{0:T(512)(128)(4,1)S(1)}, s32[96]{0:T(128)S(1)}, pred[96]{0:T(512)(128)(4,1)S(1)}, /*index=5*/s32[96]{0:T(128)S(1)}, ...), branch_computations={%region_2.5_spmd, %region_5.6_spmd} | conditional | flops 8053135360 | bytes 209198976 | solution.py:995
  34.8 8.4 %all-to-all-start.6 = ((bf16[128,128,128]{2,1,0:T(8,128)(2,1)}), bf16[128,128,128]{2,1,0:T(8,128)(2,1)}, u32[]{:S(2)}, u32[]{:S(2)}) async-start(bf16[128,128,128]{2,1,0:T(8,128)(2,1)} %get-tuple-element.76), calls=%async_computation.6 | async-start | bytes 8388608 | tf_op jit(solution)/shard_map/cond/branch_1_fun/all_to_all | solution.py:313
  44.6 25.1 %branch_1_fun.8 = (bf16[128,256,128]{2,1,0:T(8,128)(2,1)}, f32[8,256,128]{2,1,0:T(8,128)}) custom-call(s32[8,128]{1,0:T(8,128)S(1)} %get-tuple-element.68.plan_ref, s32[4,96]{1,0:T(4,128)} %add_add_fusion.slots_ref, bf16[8,256,128]{2,1,0:T(8,128)(2,1)S(1)} %copy-done.1, bf16[96,256,256]{2,1,0:T(8,128)(2,1)} %get-tuple-element.78.tiles_ref), custom_call_target="tpu_custom_call" | custom-call | flops 2415919104 | bytes 25165824 | tf_op jit(solution)/shard_map/cond/branch_1_fun/pallas_call | solution.py:527
  69.7 23.7 %all-to-all-done.6.came_ref.first_ref = bf16[128,128,128]{2,1,0:T(8,128)(2,1)} async-done(((bf16[128,128,128]{2,1,0:T(8,128)(2,1)}), bf16[128,128,128]{2,1,0:T(8,128)(2,1)}, u32[]{:S(2)}, u32[]{:S(2)}) %all-to-all-start.6) | async-done | bytes 4194336 | tf_op jit(solution)/shard_map/cond/branch_1_fun/all_to_all | solution.py:313
  93.4 5.6 %branch_1_fun.9 = bf16[128,256,128]{2,1,0:T(8,128)(2,1)} custom-call(s32[8,128]{1,0:T(8,128)S(1)} %get-tuple-element.68.plan_ref, bf16[128,128,128]{2,1,0:T(8,128)(2,1)} %all-to-all-done.6.came_ref.first_ref, bf16[128,256,128]{2,1,0:T(8,128)(2,1)} %get-tuple-element.81._), custom_call_target="tpu_custom_call", output_to_operand_aliasing={{}: (2, {})} | custom-call | tf_op jit(solution)/shard_map/cond/branch_1_fun/pallas_call | solution.py:618
  99.1 8.4 %all-to-all-start.7 = ((bf16[128,256,128]{2,1,0:T(8,128)(2,1)}), bf16[128,256,128]{2,1,0:T(8,128)(2,1)}, u32[]{:S(2)}, u32[]{:S(2)}) async-start(bf16[128,256,128]{2,1,0:T(8,128)(2,1)} %branch_1_fun.9), calls=%async_computation.7 | async-start | bytes 16777216 | tf_op jit(solution)/shard_map/cond/branch_1_fun/all_to_all | solution.py:313
  107.5 7.6 %branch_1_fun.10.start_ref = f32[8,256,128]{2,1,0:T(8,128)} custom-call(s32[8,128]{1,0:T(8,128)S(1)} %get-tuple-element.68.plan_ref, s32[4,96]{1,0:T(4,128)} %add_add_fusion.slots_ref, bf16[128,128,128]{2,1,0:T(8,128)(2,1)} %all-to-all-done.6.came_ref.first_ref, bf16[96,256,256]{2,1,0:T(8,128)(2,1)} %get-tuple-element.78.tiles_ref, ...), custom_call_target="tpu_custom_call" | custom-call | flops 805306368 | bytes 12582912 | tf_op jit(solution)/shard_map/cond/branch_1_fun/pallas_call | solution.py:662
  115.1 97.2 %all-to-all-done.7.second_ref = bf16[128,256,128]{2,1,0:T(8,128)(2,1)} async-done(((bf16[128,256,128]{2,1,0:T(8,128)(2,1)}), bf16[128,256,128]{2,1,0:T(8,128)(2,1)}, u32[]{:S(2)}, u32[]{:S(2)}) %all-to-all-start.7) | async-done | bytes 8388640 | tf_op jit(solution)/shard_map/cond/branch_1_fun/all_to_all | solution.py:313
  212.3 17.2 %branch_1_fun.11 = (bf16[8,256,256]{2,1,0:T(8,128)(2,1)}, bf16[8,256,128]{2,1,0:T(8,128)(2,1)}, bf16[128,144,128]{2,1,0:T(8,128)(2,1)}) custom-call(s32[8,128]{1,0:T(8,128)S(1)} %get-tuple-element.68.plan_ref, s32[4,96]{1,0:T(4,128)} %add_add_fusion.slots_ref, bf16[128,256,128]{2,1,0:T(8,128)(2,1)} %all-to-all-done.7.second_ref, ...), custom_call_target="tpu_custom_call" | custom-call | tf_op jit(solution)/shard_map/cond/branch_1_fun/pallas_call | solution.py:834
  229.5 8.5 %all-to-all-start.8 = ((bf16[128,144,128]{2,1,0:T(8,128)(2,1)}), bf16[128,144,128]{2,1,0:T(8,128)(2,1)}, u32[]{:S(2)}, u32[]{:S(2)}) async-start(bf16[128,144,128]{2,1,0:T(8,128)(2,1)} %get-tuple-element.86), calls=%async_computation.8 | async-start | bytes 9437184 | tf_op jit(solution)/shard_map/cond/branch_1_fun/all_to_all | solution.py:313
  238.0 25.3 %branch_1_fun.12 = (bf16[128,272,128]{2,1,0:T(8,128)(2,1)}, f32[8,256,128]{2,1,0:T(8,128)}) custom-call(s32[8,128]{1,0:T(8,128)S(1)} %get-tuple-element.68.plan_ref, s32[4,96]{1,0:T(4,128)} %add_add_fusion.slots_ref, bf16[8,256,128]{2,1,0:T(8,128)(2,1)} %get-tuple-element.87.blocks_ref, bf16[96,256,256]{2,1,0:T(8,128)(2,1)} %get-tuple-element.78.tiles_ref), custom_call_target="tpu_custom_call" | custom-call | flops 2415919104 | bytes 25165824 | tf_op jit(solution)/shard_map/cond/branch_1_fun/pallas_call | solution.py:527
  263.3 30.9 %all-to-all-done.8.came_ref.first_ref = bf16[128,144,128]{2,1,0:T(8,128)(2,1)} async-done(((bf16[128,144,128]{2,1,0:T(8,128)(2,1)}), bf16[128,144,128]{2,1,0:T(8,128)(2,1)}, u32[]{:S(2)}, u32[]{:S(2)}) %all-to-all-start.8) | async-done | bytes 4718624 | tf_op jit(solution)/shard_map/cond/branch_1_fun/all_to_all | solution.py:313
  294.2 6.0 %branch_1_fun.13 = bf16[128,272,128]{2,1,0:T(8,128)(2,1)} custom-call(s32[8,128]{1,0:T(8,128)S(1)} %get-tuple-element.68.plan_ref, bf16[128,144,128]{2,1,0:T(8,128)(2,1)} %all-to-all-done.8.came_ref.first_ref, bf16[128,272,128]{2,1,0:T(8,128)(2,1)} %get-tuple-element.90._), custom_call_target="tpu_custom_call", output_to_operand_aliasing={{}: (2, {})} | custom-call | tf_op jit(solution)/shard_map/cond/branch_1_fun/pallas_call | solution.py:618
  300.3 8.7 %all-to-all-start.9 = ((bf16[128,272,128]{2,1,0:T(8,128)(2,1)}), bf16[128,272,128]{2,1,0:T(8,128)(2,1)}, u32[]{:S(2)}, u32[]{:S(2)}) async-start(bf16[128,272,128]{2,1,0:T(8,128)(2,1)} %branch_1_fun.13), calls=%async_computation.9 | async-start | bytes 17825792 | tf_op jit(solution)/shard_map/cond/branch_1_fun/all_to_all | solution.py:313
  309.0 7.6 %branch_1_fun.14.start_ref = f32[8,256,128]{2,1,0:T(8,128)} custom-call(s32[8,128]{1,0:T(8,128)S(1)} %get-tuple-element.68.plan_ref, s32[4,96]{1,0:T(4,128)} %add_add_fusion.slots_ref, bf16[128,144,128]{2,1,0:T(8,128)(2,1)} %all-to-all-done.8.came_ref.first_ref, bf16[96,256,256]{2,1,0:T(8,128)(2,1)} %get-tuple-element.78.tiles_ref, ...), custom_call_target="tpu_custom_call" | custom-call | flops 805306368 | bytes 12582912 | tf_op jit(solution)/shard_map/cond/branch_1_fun/pallas_call | solution.py:662
  316.7 107.0 %all-to-all-done.9.second_ref = bf16[128,272,128]{2,1,0:T(8,128)(2,1)} async-done(((bf16[128,272,128]{2,1,0:T(8,128)(2,1)}), bf16[128,272,128]{2,1,0:T(8,128)(2,1)}, u32[]{:S(2)}, u32[]{:S(2)}) %all-to-all-start.9) | async-done | bytes 8912928 | tf_op jit(solution)/shard_map/cond/branch_1_fun/all_to_all | solution.py:313
  423.7 9.0 %branch_1_fun.15 = (bf16[8,256,128]{2,1,0:T(8,128)(2,1)}, f32[128,256]{1,0:T(8,128)}) custom-call(s32[8,128]{1,0:T(8,128)S(1)} %get-tuple-element.68.plan_ref, s32[4,96]{1,0:T(4,128)} %add_add_fusion.slots_ref, bf16[128,272,128]{2,1,0:T(8,128)(2,1)} %all-to-all-done.9.second_ref, bf16[96,256,256]{2,1,0:T(8,128)(2,1)} %get-tuple-element.78.tiles_ref, ...), custom_call_target="tpu_custom_call" | custom-call | tf_op jit(solution)/shard_map/cond/branch_1_fun/pallas_call | solution.py:905
  (15 shorter events, 2.0 us)
Async XLA Ops:
  3.5 17.1 %all-to-all-start.10 = ((s32[128,1,128]{2,1,0:T(1,128)}), s32[128,1,128]{2,1,0:T(1,128)S(1)}, u32[]{:S(2)}, u32[]{:S(2)}) async-start(s32[128,1,128]{2,1,0:T(1,128)} %broadcast_in_dim.68), calls=%async_computation.10 | async-start | bytes 131072 | tf_op jit(solution)/shard_map/all_to_all | solution.py:313
  20.6 0.6 copy-start.6
  34.7 9.8 %copy-start.1 = (bf16[8,256,128]{2,1,0:T(8,128)(2,1)S(1)}, bf16[8,256,128]{2,1,0:T(8,128)(2,1)}, u32[]{:S(2)}) copy-start(bf16[8,256,128]{2,1,0:T(8,128)(2,1)} %get-tuple-element.77.blocks_ref) | copy-start | bytes 1572868 | tf_op jit(solution)/shard_map/cond
  34.8 58.7 %all-to-all-start.6 = ((bf16[128,128,128]{2,1,0:T(8,128)(2,1)}), bf16[128,128,128]{2,1,0:T(8,128)(2,1)}, u32[]{:S(2)}, u32[]{:S(2)}) async-start(bf16[128,128,128]{2,1,0:T(8,128)(2,1)} %get-tuple-element.76), calls=%async_computation.6 | async-start | bytes 8388608 | tf_op jit(solution)/shard_map/cond/branch_1_fun/all_to_all | solution.py:313
  99.1 113.2 %all-to-all-start.7 = ((bf16[128,256,128]{2,1,0:T(8,128)(2,1)}), bf16[128,256,128]{2,1,0:T(8,128)(2,1)}, u32[]{:S(2)}, u32[]{:S(2)}) async-start(bf16[128,256,128]{2,1,0:T(8,128)(2,1)} %branch_1_fun.9), calls=%async_computation.7 | async-start | bytes 16777216 | tf_op jit(solution)/shard_map/cond/branch_1_fun/all_to_all | solution.py:313
  107.5 104.8 %copy-start.3 = (bf16[8,256,256]{2,1,0:T(8,128)(2,1)S(1)}, bf16[8,256,256]{2,1,0:T(8,128)(2,1)}, u32[]{:S(2)}) copy-start(bf16[8,256,256]{2,1,0:T(8,128)(2,1)} %get-tuple-element.84.cotangent_ref) | copy-start | bytes 3145732 | tf_op jit(solution)/shard_map/cond
  107.5 104.8 %copy-start.5 = (bf16[128,256]{1,0:T(8,128)(2,1)S(1)}, bf16[128,256]{1,0:T(8,128)(2,1)}, u32[]{:S(2)}) copy-start(bf16[128,256]{1,0:T(8,128)(2,1)} %get-tuple-element.83.weight_ref) | copy-start | bytes 196612 | tf_op jit(solution)/shard_map/cond
  229.5 64.8 %all-to-all-start.8 = ((bf16[128,144,128]{2,1,0:T(8,128)(2,1)}), bf16[128,144,128]{2,1,0:T(8,128)(2,1)}, u32[]{:S(2)}, u32[]{:S(2)}) async-start(bf16[128,144,128]{2,1,0:T(8,128)(2,1)} %get-tuple-element.86), calls=%async_computation.8 | async-start | bytes 9437184 | tf_op jit(solution)/shard_map/cond/branch_1_fun/all_to_all | solution.py:313
  300.3 123.4 %all-to-all-start.9 = ((bf16[128,272,128]{2,1,0:T(8,128)(2,1)}), bf16[128,272,128]{2,1,0:T(8,128)(2,1)}, u32[]{:S(2)}, u32[]{:S(2)}) async-start(bf16[128,272,128]{2,1,0:T(8,128)(2,1)} %branch_1_fun.13), calls=%async_computation.9 | async-start | bytes 17825792 | tf_op jit(solution)/shard_map/cond/branch_1_fun/all_to_all | solution.py:313

commit v3 on v2

--- a/solution.py
+++ b/solution.py
@@ -313,12 +313,12 @@
     return lax.all_to_all(values, "nodes", split_axis=0, concat_axis=0, tiled=True)
 
 
-ASKED, VIA, RELAYED, CAME_VIA, WANTED, FITS = range(6)
+ASKED, SOURCE, RELAYED, CAME_VIA, WANTED, FITS = range(6)
 OPEN = -2
 
 
 def plan_kernel(
-    me_ref, wanted_ref, blocks_ref, plan_ref, out_ref, free_ref, rows_ref, columns_ref, known_ref, sems
+    me_ref, wanted_ref, blocks_ref, plan_ref, out_ref, free_ref, columns_ref, known_ref, sems
 ):
     peers = wanted_ref.shape[0]
     groups = peers // 8
@@ -376,26 +376,32 @@
         (jnp.int32(0), left_open(routes), routes, spares),
     )
     route = jnp.concatenate(routes, 0)
-    rows_ref[...] = route
-    columns_ref[...] = route.astype(jnp.float32).T.astype(jnp.int32)
-    plan_ref[VIA : VIA + 1, :] = rows_ref[pl.ds(me, 1), :]
+    columns = route.astype(jnp.float32).T.astype(jnp.int32)
+    columns_ref[...] = columns
     plan_ref[CAME_VIA : CAME_VIA + 1, :] = columns_ref[pl.ds(me, 1), :]
     plan_ref[RELAYED : RELAYED + 1, :] = jnp.max(
         jnp.where(route == me, u_ids, -1), axis=0, keepdims=True
     )
     columns_ref[...] = raw.astype(jnp.float32).T.astype(jnp.int32)
-    plan_ref[ASKED : ASKED + 1, :] = columns_ref[pl.ds(me, 1), :]
+    asked = columns_ref[pl.ds(me, 1), :]
+    plan_ref[ASKED : ASKED + 1, :] = asked
+    lanes = lax.broadcasted_iota(jnp.int32, raw.shape, 1)
+    my_column = lanes == me
+    my_vias = jnp.sum(jnp.where(my_column, columns, 0).astype(jnp.float32), 1, keepdims=True)
+    my_asked = jnp.sum(jnp.where(my_column, raw, 0).astype(jnp.float32), 1, keepdims=True)
+    second = jnp.where(my_vias == lanes.astype(jnp.float32), 2.0 * my_asked + 1.0, 0.0)
+    second = jnp.max(second, axis=0, keepdims=True).astype(jnp.int32)
+    pieces = 2 * blocks_ref.shape[0]
+    plan_ref[SOURCE : SOURCE + 1, :] = jnp.where(asked >= 0, 2 * asked, second) & (pieces - 1)
     plan_ref[WANTED : WANTED + 1, :] = wanted_ref[pl.ds(me, 1), :]
     twice = jnp.sum((raw >= TWICE).astype(jnp.float32)).astype(jnp.int32)
     fits = jnp.where((left == 0) & (twice == 0), 1, 0)
     plan_ref[FITS:, :] = jnp.full((plan_ref.shape[0] - FITS, peers), fits, jnp.int32)
-    tell = pltpu.make_async_copy(plan_ref, known_ref, sems.at[2 * peers])
+    tell = pltpu.make_async_copy(plan_ref, known_ref, sems.at[0])
     tell.start()
     tell.wait()
-
-    @pl.when(fits > 0)
-    def _():
-        send_first(known_ref, blocks_ref, out_ref, sems)
+    start_first(known_ref, blocks_ref, out_ref, sems.at[1])
+    wait_first(out_ref, blocks_ref.shape[1] // 2, sems.at[1])
 
 
 def make_plan(myself, wanted, blocks):
@@ -412,9 +418,8 @@
             scratch_shapes=[
                 pltpu.VMEM((peers, 8, peers), jnp.int32),
                 square,
-                square,
                 pltpu.SMEM((8, peers), jnp.int32),
-                pltpu.SemaphoreType.DMA((2 * peers + 1,)),
+                pltpu.SemaphoreType.DMA((2,)),
             ],
         ),
         out_shape=[
@@ -433,45 +438,22 @@
     lax.fori_loop(0, peers, step, 0, unroll=8)
 
 
-def send_first(plan_ref, blocks_ref, out_ref, sems):
-    peers = plan_ref.shape[1]
+def start_first(plan_ref, blocks_ref, out_ref, sem):
     half = blocks_ref.shape[1] // 2
 
-    def direct(q):
-        block = jnp.maximum(plan_ref[ASKED, q], 0)
-        return pltpu.make_async_copy(
-            blocks_ref.at[block, pl.ds(0, half)], out_ref.at[q, pl.ds(0, half)], sems.at[q]
-        )
-
-    def relayed(q):
-        block = jnp.maximum(plan_ref[ASKED, q], 0)
-        via = jnp.maximum(plan_ref[VIA, q], 0)
-        return pltpu.make_async_copy(
-            blocks_ref.at[block, pl.ds(half, half)],
-            out_ref.at[via, pl.ds(0, half)],
-            sems.at[peers + q],
-        )
-
     def start(q):
-        @pl.when(plan_ref[ASKED, q] >= 0)
-        def _():
-            direct(q).start()
-
-        @pl.when(plan_ref[VIA, q] >= 0)
-        def _():
-            relayed(q).start()
-
-    def wait(q):
-        @pl.when(plan_ref[ASKED, q] >= 0)
-        def _():
-            direct(q).wait()
-
-        @pl.when(plan_ref[VIA, q] >= 0)
-        def _():
-            relayed(q).wait()
-
-    each_peer(peers, start)
-    each_peer(peers, wait)
+        source = plan_ref[SOURCE, q]
+        offset = pl.multiple_of((source & 1) * half, half)
+        pltpu.make_async_copy(
+            blocks_ref.at[source >> 1, pl.ds(offset, half)], out_ref.at[q, pl.ds(0, half)], sem
+        ).start()
+
+    each_peer(plan_ref.shape[1], start)
+
+
+def wait_first(out_ref, half, sem):
+    whole_part = out_ref.at[:, pl.ds(0, half)]
+    pltpu.make_async_copy(whole_part, whole_part, sem).wait()
 
 
 def tiles_spec(rows):
@@ -555,26 +537,18 @@
     peers = plan_ref.shape[1]
     half = came_ref.shape[1] - (EXTRA if grad_refs else 0)
 
-    def take(q):
+    take = pltpu.make_async_copy(came_ref.at[:, pl.ds(0, half)], held_ref, sems.at[peers])
+    take.start()
+
+    def give(q):
         source = jnp.maximum(plan_ref[RELAYED, q], 0)
         return pltpu.make_async_copy(
-            came_ref.at[source, pl.ds(0, half)], held_ref.at[q], sems.at[q]
+            held_ref.at[source], out_ref.at[q, pl.ds(half, half)], sems.at[q]
         )
-
-    def give(q):
-        return pltpu.make_async_copy(
-            held_ref.at[q], out_ref.at[q, pl.ds(half, half)], sems.at[peers + q]
-        )
-
-    def start(q):
-        @pl.when(plan_ref[RELAYED, q] >= 0)
-        def _():
-            take(q).start()
 
     def turn(q):
         @pl.when(plan_ref[RELAYED, q] >= 0)
         def _():
-            take(q).wait()
             give(q).start()
 
     def wait(q):
@@ -585,10 +559,11 @@
     if grad_refs:
         (staged_ref,) = grad_refs
         bring = pltpu.make_async_copy(
-            came_ref.at[:, pl.ds(half, EXTRA)], staged_ref, sems.at[2 * peers]
+            came_ref.at[:, pl.ds(half, EXTRA)], staged_ref, sems.at[peers + 1]
         )
         bring.start()
-    each_peer(peers, start)
+    take.wait()
+    each_peer(peers, turn)
     if grad_refs:
         bring.wait()
         sums = jnp.sum(staged_ref[...].astype(jnp.float32), axis=0)
@@ -597,11 +572,9 @@
         packed = jnp.concatenate(parts + [jnp.zeros((EXTRA - 6, own.shape[1]), jnp.float32)], 0)
         staged_ref[...] = jnp.broadcast_to(packed[None], staged_ref.shape).astype(jnp.bfloat16)
         put = pltpu.make_async_copy(
-            staged_ref, out_ref.at[:, pl.ds(2 * half, EXTRA)], sems.at[2 * peers + 1]
+            staged_ref, out_ref.at[:, pl.ds(2 * half, EXTRA)], sems.at[peers + 2]
         )
         put.start()
-    each_peer(peers, turn)
-    if grad_refs:
         put.wait()
     each_peer(peers, wait)
 
@@ -610,7 +583,7 @@
     peers, _, width = came.shape
     scratch = [
         pltpu.VMEM((peers, came.shape[1] - (EXTRA if with_grad else 0), width), came.dtype),
-        pltpu.SemaphoreType.DMA((2 * peers + 2,)),
+        pltpu.SemaphoreType.DMA((peers + 3,)),
     ]
     if with_grad:
         scratch.append(pltpu.VMEM((peers, EXTRA, width), jnp.bfloat16))
@@ -690,7 +663,7 @@
         pltpu.VMEM((start.shape[0] + 1, rows, width), jnp.float32),
         pltpu.VMEM(second.shape, second.dtype),
         pltpu.VMEM((slot_total, rows, rows // 2), tile_values.dtype),
-        pltpu.SemaphoreType.DMA((PARTS + slot_total // GROUP,)),
+        pltpu.SemaphoreType.DMA((PARTS + slot_total // GROUP + 1,)),
     ]
 
 
@@ -710,16 +683,20 @@
             tiles_ref.at[piece, :, pl.ds(half, half)], held_ref.at[piece], sems.at[PARTS + group]
         )
 
+    groups = slot_total // GROUP
+    begin = pltpu.make_async_copy(
+        start_ref, total_ref.at[pl.ds(0, locals_)], sems.at[PARTS + groups]
+    )
+    begin.start()
     for part in range(PARTS):
         landing(part).start()
-    groups = slot_total // GROUP
     for group in range(groups):
 
         @pl.when(group <= slots_ref[LAST, 0])
         def _():
             holding(group).start()
 
-    total_ref[pl.ds(0, locals_)] = start_ref[...]
+    begin.wait()
 
     def add(q, carry):
         block = plan_ref[ASKED, q]
@@ -775,8 +752,14 @@
     grad_ref,
     rows_ref,
     staged_ref,
+    gradient_ref,
+    result_ref,
+    back_ref,
     sems,
 ):
+    locals_ = total_ref.shape[0] - 1
+    bring = pltpu.make_async_copy(cotangent_ref, gradient_ref, sems.at[2 * locals_])
+    bring.start()
     late_sums(
         plan_ref,
         slots_ref,
@@ -793,24 +776,34 @@
     width = upstream_ref.shape[2]
     weight = weight_ref[...]
     grad_ref[...] = jnp.zeros_like(grad_ref)
+    bring.wait()
+
+    def give(k):
+        return (
+            pltpu.make_async_copy(result_ref.at[k], hidden_ref.at[k], sems.at[k]),
+            pltpu.make_async_copy(back_ref.at[k], upstream_ref.at[k], sems.at[locals_ + k]),
+        )
 
     def block_step(k, carry):
         aggregated = total_ref[k].astype(jnp.bfloat16)
         preact = jnp.dot(aggregated, weight, preferred_element_type=jnp.float32)
         sigma = 1.0 / (1.0 + jnp.exp(-preact))
-        hidden_ref[k] = (preact * sigma).astype(jnp.bfloat16)
+        result_ref[k] = (preact * sigma).astype(jnp.bfloat16)
         delta = (
-            cotangent_ref[k].astype(jnp.float32) * sigma * (1.0 + preact * (1.0 - sigma))
+            gradient_ref[k].astype(jnp.float32) * sigma * (1.0 + preact * (1.0 - sigma))
         ).astype(jnp.bfloat16)
         grad_ref[...] += lax.dot_general(
             aggregated, delta, (((0,), (0,)), ((), ())), preferred_element_type=jnp.float32
         )
-        upstream_ref[k] = lax.dot_general(
+        back_ref[k] = lax.dot_general(
             delta, weight, (((1,), (1,)), ((), ())), preferred_element_type=jnp.float32
         ).astype(jnp.bfloat16)
+        for copy in give(k):
+            copy.start()
         return carry
 
-    lax.fori_loop(0, cotangent_ref.shape[0], block_step, 0, unroll=2)
+    lax.fori_loop(0, locals_, block_step, 0, unroll=2)
+    start_first(plan_ref, back_ref, out_ref, sems.at[2 * locals_ + 1])
     for side in range(2):
         parts = three_parts(grad_ref[:, side * width : (side + 1) * width])
         for at, part in enumerate(parts):
@@ -818,9 +811,14 @@
     for at in range(6, EXTRA):
         rows_ref[:, at, :] = jnp.zeros((peers, width), jnp.float32)
     staged_ref[...] = rows_ref[...].astype(jnp.bfloat16)
-    put = pltpu.make_async_copy(staged_ref, out_ref.at[:, pl.ds(half, EXTRA)], sems.at[2 * peers])
+    put = pltpu.make_async_copy(
+        staged_ref, out_ref.at[:, pl.ds(half, EXTRA)], sems.at[2 * locals_ + 2]
+    )
     put.start()
-    send_first(plan_ref, upstream_ref, out_ref, sems)
+    for k in range(locals_):
+        for copy in give(k):
+            copy.wait()
+    wait_first(out_ref, half, sems.at[2 * locals_ + 1])
     put.wait()
 
 
@@ -836,20 +834,17 @@
         grid_spec=pltpu.PrefetchScalarGridSpec(
             num_scalar_prefetch=2,
             grid=(1,),
-            in_specs=[
-                anywhere,
-                anywhere,
-                whole(*start.shape),
-                whole(width, hid),
-                whole(locals_, rows, hid),
-            ],
-            out_specs=[whole(locals_, rows, hid), whole(locals_, rows, width), anywhere],
+            in_specs=[anywhere, anywhere, anywhere, whole(width, hid), anywhere],
+            out_specs=[anywhere, anywhere, anywhere],
             scratch_shapes=late_scratch(second, tile_values, start)
             + [
                 pltpu.VMEM((width, hid), jnp.float32),
                 pltpu.VMEM((peers, EXTRA, width), jnp.float32),
                 pltpu.VMEM((peers, EXTRA, width), jnp.bfloat16),
-                pltpu.SemaphoreType.DMA((2 * peers + 1,)),
+                pltpu.VMEM((locals_, rows, hid), jnp.bfloat16),
+                pltpu.VMEM((locals_, rows, hid), jnp.bfloat16),
+                pltpu.VMEM((locals_, rows, width), jnp.bfloat16),
+                pltpu.SemaphoreType.DMA((2 * locals_ + 3,)),
             ],
         ),
         out_shape=[
@@ -907,7 +902,7 @@
         grid_spec=pltpu.PrefetchScalarGridSpec(
             num_scalar_prefetch=2,
             grid=(1,),
-            in_specs=[anywhere, anywhere, whole(*start.shape)],
+            in_specs=[anywhere, anywhere, anywhere],
             out_specs=[whole(locals_, rows, width), whole(peers, 2 * width)],
             scratch_shapes=late_scratch(second, tile_values, start)
             + [pltpu.VMEM((peers, EXTRA, width), jnp.float32)],

time: 434 us -> 423 us (0.975)
  waiting for transfers between devices: 265 us -> 253 us
    all_to_all x5, waiting for transfers between devices: 265 us -> 253 us  [exchange(): lax.all_to_all(values, 'nodes', split_axis=0, concat_axis=0, tiled=True)]
    pallas_call x2, Pallas kernels: 50.4 us -> 58.8 us  [own_products(): pl.pallas_call(products_kernel, grid_spec=pltpu.PrefetchScalarGridSpec(nu...]
    pallas_call x1, Pallas kernels: 17.2 us -> 12 us  [layer(): pl.pallas_call(layer_kernel, grid_spec=pltpu.PrefetchScalarGridSpec(num_s...]
    pallas_call x1, Pallas kernels: 12.3 us -> 7.5 us  [make_plan(): pl.pallas_call(plan_kernel, grid_spec=pltpu.PrefetchScalarGridSpec(num_sc...]
  transfers between devices with their start and end apart: 5 -> 5, of which waited for: 5 -> 5; matrix products, arithmetic and copies ran while one was open for 0% -> 0% of each run, Pallas kernels for 15% -> 18%
where the time goes in v3:
time: 423 us; the launch traced here: 421 us
  waiting for transfers between devices  253 us (60%)
  Pallas kernels  115 us (27%)
  starting transfers between devices  45.5 us (11%)
    all_to_all x5, waiting for transfers between devices, exchange(): lax.all_to_all(values, 'nodes', split_axis=0, concat_axis=0, tiled=True)  253 us
    pallas_call x2, Pallas kernels, own_products(): pl.pallas_call(products_kernel, grid_spec=pltpu.PrefetchScalarGridSpec(nu...  58.8 us
    all_to_all x5, starting transfers between devices, exchange(): lax.all_to_all(values, 'nodes', split_axis=0, concat_axis=0, tiled=True)  45.5 us
    pallas_call x2, Pallas kernels, early_products(): pl.pallas_call(early_kernel, grid_spec=pltpu.PrefetchScalarGridSpec(num_s...  17.5 us
    pallas_call x1, Pallas kernels, layer(): pl.pallas_call(layer_kernel, grid_spec=pltpu.PrefetchScalarGridSpec(num_s...  12 us
    pallas_call x2, Pallas kernels, relay(): pl.pallas_call(relay_kernel, grid_spec=pltpu.PrefetchScalarGridSpec(num_s...  10.3 us
    pallas_call x1, Pallas kernels, last(): pl.pallas_call(functools.partial(last_kernel, scale), grid_spec=pltpu.Pre...  8.61 us
  transfers between devices with their start and end apart: 5, of which 5 were waited for; matrix products, arithmetic and copies ran while one was open for 0% of the time, Pallas kernels for 18%

profile of v3, /device:TPU:38, one launch (start us, length us, event | category | flops | bytes accessed | tf_op | source)
XLA Modules:
  0.0 421.5 jit_solution(9294213855041780422)
XLA Ops:
  1.3 0.7 and_select_fusion.2
  2.0 0.7 compare_and_fusion
  2.8 0.7 broadcast_in_dim.68
  3.5 10.2 %all-to-all-start.10 = ((s32[128,1,128]{2,1,0:T(1,128)}), s32[128,1,128]{2,1,0:T(1,128)S(1)}, u32[]{:S(2)}, u32[]{:S(2)}) async-start(s32[128,1,128]{2,1,0:T(1,128)} %broadcast_in_dim.68), calls=%async_computation.10 | async-start | bytes 131072 | tf_op jit(solution)/shard_map/all_to_all | solution.py:313
  13.7 0.7 clamp_bitcast_fusion
  14.4 6.3 %all-to-all-done.10 = s32[128,1,128]{2,1,0:T(1,128)S(1)} async-done(((s32[128,1,128]{2,1,0:T(1,128)}), s32[128,1,128]{2,1,0:T(1,128)S(1)}, u32[]{:S(2)}, u32[]{:S(2)}) %all-to-all-start.10) | async-done | bytes 65568 | tf_op jit(solution)/shard_map/all_to_all | solution.py:313
  21.2 7.5 %shard_map.85 = (s32[8,128]{1,0:T(8,128)S(1)}, bf16[128,128,128]{2,1,0:T(8,128)(2,1)}) custom-call(s32[1]{0:T(128)} %bitcast.7.me_ref, s32[128,128]{1,0:T(8,128)} %bitcast.44, bf16[8,256,128]{2,1,0:T(8,128)(2,1)} %bitcast.37), custom_call_target="tpu_custom_call" | custom-call | tf_op jit(solution)/shard_map/pallas_call | solution.py:411
  29.9 391.4 %conditional.1 = (bf16[8,256,256]{2,1,0:T(8,128)(2,1)}, f32[128,256]{1,0:T(8,128)}, bf16[2048,128]{1,0:T(8,128)(2,1)}) conditional(s32[]{:T(128)} %bitcast.12, (s32[8,128]{1,0:T(8,128)S(1)}, s32[96]{0:T(128)S(1)}, pred[96]{0:T(512)(128)(4,1)S(1)}, s32[96]{0:T(128)S(1)}, pred[96]{0:T(512)(128)(4,1)S(1)}, /*index=5*/s32[96]{0:T(128)S(1)}, ...), branch_computations={%region_2.5_spmd, %region_5.6_spmd} | conditional | flops 8053135360 | bytes 209198976 | solution.py:990
  30.0 8.4 %all-to-all-start.6 = ((bf16[128,128,128]{2,1,0:T(8,128)(2,1)}), bf16[128,128,128]{2,1,0:T(8,128)(2,1)}, u32[]{:S(2)}, u32[]{:S(2)}) async-start(bf16[128,128,128]{2,1,0:T(8,128)(2,1)} %get-tuple-element.76), calls=%async_computation.6 | async-start | bytes 8388608 | tf_op jit(solution)/shard_map/cond/branch_1_fun/all_to_all | solution.py:313
  39.8 29.3 %branch_1_fun.8 = (bf16[128,256,128]{2,1,0:T(8,128)(2,1)}, f32[8,256,128]{2,1,0:T(8,128)}) custom-call(s32[8,128]{1,0:T(8,128)S(1)} %get-tuple-element.68.plan_ref, s32[4,96]{1,0:T(4,128)} %add_add_fusion.slots_ref, bf16[8,256,128]{2,1,0:T(8,128)(2,1)S(1)} %copy-done.1, bf16[96,256,256]{2,1,0:T(8,128)(2,1)} %get-tuple-element.78.tiles_ref), custom_call_target="tpu_custom_call" | custom-call | flops 2415919104 | bytes 25165824 | tf_op jit(solution)/shard_map/cond/branch_1_fun/pallas_call | solution.py:509
  69.1 19.6 %all-to-all-done.6.came_ref.first_ref = bf16[128,128,128]{2,1,0:T(8,128)(2,1)} async-done(((bf16[128,128,128]{2,1,0:T(8,128)(2,1)}), bf16[128,128,128]{2,1,0:T(8,128)(2,1)}, u32[]{:S(2)}, u32[]{:S(2)}) %all-to-all-start.6) | async-done | bytes 4194336 | tf_op jit(solution)/shard_map/cond/branch_1_fun/all_to_all | solution.py:313
  88.7 4.8 %branch_1_fun.9 = bf16[128,256,128]{2,1,0:T(8,128)(2,1)} custom-call(s32[8,128]{1,0:T(8,128)S(1)} %get-tuple-element.68.plan_ref, bf16[128,128,128]{2,1,0:T(8,128)(2,1)} %all-to-all-done.6.came_ref.first_ref, bf16[128,256,128]{2,1,0:T(8,128)(2,1)} %get-tuple-element.81._), custom_call_target="tpu_custom_call", output_to_operand_aliasing={{}: (2, {})} | custom-call | tf_op jit(solution)/shard_map/cond/branch_1_fun/pallas_call | solution.py:591
  93.5 8.7 %all-to-all-start.7 = ((bf16[128,256,128]{2,1,0:T(8,128)(2,1)}), bf16[128,256,128]{2,1,0:T(8,128)(2,1)}, u32[]{:S(2)}, u32[]{:S(2)}) async-start(bf16[128,256,128]{2,1,0:T(8,128)(2,1)} %branch_1_fun.9), calls=%async_computation.7 | async-start | bytes 16777216 | tf_op jit(solution)/shard_map/cond/branch_1_fun/all_to_all | solution.py:313
  102.2 8.7 %branch_1_fun.10.start_ref = f32[8,256,128]{2,1,0:T(8,128)} custom-call(s32[8,128]{1,0:T(8,128)S(1)} %get-tuple-element.68.plan_ref, s32[4,96]{1,0:T(4,128)} %add_add_fusion.slots_ref, bf16[128,128,128]{2,1,0:T(8,128)(2,1)} %all-to-all-done.6.came_ref.first_ref, bf16[96,256,256]{2,1,0:T(8,128)(2,1)} %get-tuple-element.78.tiles_ref, ...), custom_call_target="tpu_custom_call" | custom-call | flops 805306368 | bytes 12582912 | tf_op jit(solution)/shard_map/cond/branch_1_fun/pallas_call | solution.py:635
  110.9 95.0 %all-to-all-done.7.second_ref = bf16[128,256,128]{2,1,0:T(8,128)(2,1)} async-done(((bf16[128,256,128]{2,1,0:T(8,128)(2,1)}), bf16[128,256,128]{2,1,0:T(8,128)(2,1)}, u32[]{:S(2)}, u32[]{:S(2)}) %all-to-all-start.7) | async-done | bytes 8388640 | tf_op jit(solution)/shard_map/cond/branch_1_fun/all_to_all | solution.py:313
  205.9 12.0 %branch_1_fun.11 = (bf16[8,256,256]{2,1,0:T(8,128)(2,1)}, bf16[8,256,128]{2,1,0:T(8,128)(2,1)}, bf16[128,144,128]{2,1,0:T(8,128)(2,1)}) custom-call(s32[8,128]{1,0:T(8,128)S(1)} %get-tuple-element.68.plan_ref, s32[4,96]{1,0:T(4,128)} %add_add_fusion.slots_ref, bf16[128,256,128]{2,1,0:T(8,128)(2,1)} %all-to-all-done.7.second_ref, ...), custom_call_target="tpu_custom_call" | custom-call | tf_op jit(solution)/shard_map/cond/branch_1_fun/pallas_call | solution.py:832
  217.9 9.3 %all-to-all-start.8 = ((bf16[128,144,128]{2,1,0:T(8,128)(2,1)}), bf16[128,144,128]{2,1,0:T(8,128)(2,1)}, u32[]{:S(2)}, u32[]{:S(2)}) async-start(bf16[128,144,128]{2,1,0:T(8,128)(2,1)} %get-tuple-element.86), calls=%async_computation.8 | async-start | bytes 9437184 | tf_op jit(solution)/shard_map/cond/branch_1_fun/all_to_all | solution.py:313
  227.2 29.5 %branch_1_fun.12 = (bf16[128,272,128]{2,1,0:T(8,128)(2,1)}, f32[8,256,128]{2,1,0:T(8,128)}) custom-call(s32[8,128]{1,0:T(8,128)S(1)} %get-tuple-element.68.plan_ref, s32[4,96]{1,0:T(4,128)} %add_add_fusion.slots_ref, bf16[8,256,128]{2,1,0:T(8,128)(2,1)} %get-tuple-element.87.blocks_ref, bf16[96,256,256]{2,1,0:T(8,128)(2,1)} %get-tuple-element.78.tiles_ref), custom_call_target="tpu_custom_call" | custom-call | flops 2415919104 | bytes 25165824 | tf_op jit(solution)/shard_map/cond/branch_1_fun/pallas_call | solution.py:509
  256.7 26.8 %all-to-all-done.8.came_ref.first_ref = bf16[128,144,128]{2,1,0:T(8,128)(2,1)} async-done(((bf16[128,144,128]{2,1,0:T(8,128)(2,1)}), bf16[128,144,128]{2,1,0:T(8,128)(2,1)}, u32[]{:S(2)}, u32[]{:S(2)}) %all-to-all-start.8) | async-done | bytes 4718624 | tf_op jit(solution)/shard_map/cond/branch_1_fun/all_to_all | solution.py:313
  283.4 5.5 %branch_1_fun.13 = bf16[128,272,128]{2,1,0:T(8,128)(2,1)} custom-call(s32[8,128]{1,0:T(8,128)S(1)} %get-tuple-element.68.plan_ref, bf16[128,144,128]{2,1,0:T(8,128)(2,1)} %all-to-all-done.8.came_ref.first_ref, bf16[128,272,128]{2,1,0:T(8,128)(2,1)} %get-tuple-element.90._), custom_call_target="tpu_custom_call", output_to_operand_aliasing={{}: (2, {})} | custom-call | tf_op jit(solution)/shard_map/cond/branch_1_fun/pallas_call | solution.py:591
  288.9 8.9 %all-to-all-start.9 = ((bf16[128,272,128]{2,1,0:T(8,128)(2,1)}), bf16[128,272,128]{2,1,0:T(8,128)(2,1)}, u32[]{:S(2)}, u32[]{:S(2)}) async-start(bf16[128,272,128]{2,1,0:T(8,128)(2,1)} %branch_1_fun.13), calls=%async_computation.9 | async-start | bytes 17825792 | tf_op jit(solution)/shard_map/cond/branch_1_fun/all_to_all | solution.py:313
  297.8 8.7 %branch_1_fun.14.start_ref = f32[8,256,128]{2,1,0:T(8,128)} custom-call(s32[8,128]{1,0:T(8,128)S(1)} %get-tuple-element.68.plan_ref, s32[4,96]{1,0:T(4,128)} %add_add_fusion.slots_ref, bf16[128,144,128]{2,1,0:T(8,128)(2,1)} %all-to-all-done.8.came_ref.first_ref, bf16[96,256,256]{2,1,0:T(8,128)(2,1)} %get-tuple-element.78.tiles_ref, ...), custom_call_target="tpu_custom_call" | custom-call | flops 805306368 | bytes 12582912 | tf_op jit(solution)/shard_map/cond/branch_1_fun/pallas_call | solution.py:635
  306.6 105.9 %all-to-all-done.9.second_ref = bf16[128,272,128]{2,1,0:T(8,128)(2,1)} async-done(((bf16[128,272,128]{2,1,0:T(8,128)(2,1)}), bf16[128,272,128]{2,1,0:T(8,128)(2,1)}, u32[]{:S(2)}, u32[]{:S(2)}) %all-to-all-start.9) | async-done | bytes 8912928 | tf_op jit(solution)/shard_map/cond/branch_1_fun/all_to_all | solution.py:313
  412.5 8.6 %branch_1_fun.15 = (bf16[8,256,128]{2,1,0:T(8,128)(2,1)}, f32[128,256]{1,0:T(8,128)}) custom-call(s32[8,128]{1,0:T(8,128)S(1)} %get-tuple-element.68.plan_ref, s32[4,96]{1,0:T(4,128)} %add_add_fusion.slots_ref, bf16[128,272,128]{2,1,0:T(8,128)(2,1)} %all-to-all-done.9.second_ref, bf16[96,256,256]{2,1,0:T(8,128)(2,1)} %get-tuple-element.78.tiles_ref, ...), custom_call_target="tpu_custom_call" | custom-call | tf_op jit(solution)/shard_map/cond/branch_1_fun/pallas_call | solution.py:900
  (15 shorter events, 2.0 us)
Async XLA Ops:
  3.5 17.1 %all-to-all-start.10 = ((s32[128,1,128]{2,1,0:T(1,128)}), s32[128,1,128]{2,1,0:T(1,128)S(1)}, u32[]{:S(2)}, u32[]{:S(2)}) async-start(s32[128,1,128]{2,1,0:T(1,128)} %broadcast_in_dim.68), calls=%async_computation.10 | async-start | bytes 131072 | tf_op jit(solution)/shard_map/all_to_all | solution.py:313
  20.6 0.6 copy-start.6
  29.9 9.8 %copy-start.1 = (bf16[8,256,128]{2,1,0:T(8,128)(2,1)S(1)}, bf16[8,256,128]{2,1,0:T(8,128)(2,1)}, u32[]{:S(2)}) copy-start(bf16[8,256,128]{2,1,0:T(8,128)(2,1)} %get-tuple-element.77.blocks_ref) | copy-start | bytes 1572868 | tf_op jit(solution)/shard_map/cond
  30.0 58.7 %all-to-all-start.6 = ((bf16[128,128,128]{2,1,0:T(8,128)(2,1)}), bf16[128,128,128]{2,1,0:T(8,128)(2,1)}, u32[]{:S(2)}, u32[]{:S(2)}) async-start(bf16[128,128,128]{2,1,0:T(8,128)(2,1)} %get-tuple-element.76), calls=%async_computation.6 | async-start | bytes 8388608 | tf_op jit(solution)/shard_map/cond/branch_1_fun/all_to_all | solution.py:313
  93.5 112.4 %all-to-all-start.7 = ((bf16[128,256,128]{2,1,0:T(8,128)(2,1)}), bf16[128,256,128]{2,1,0:T(8,128)(2,1)}, u32[]{:S(2)}, u32[]{:S(2)}) async-start(bf16[128,256,128]{2,1,0:T(8,128)(2,1)} %branch_1_fun.9), calls=%async_computation.7 | async-start | bytes 16777216 | tf_op jit(solution)/shard_map/cond/branch_1_fun/all_to_all | solution.py:313
  102.2 103.7 %copy-start.3 = (bf16[8,256,256]{2,1,0:T(8,128)(2,1)S(1)}, bf16[8,256,256]{2,1,0:T(8,128)(2,1)}, u32[]{:S(2)}) copy-start(bf16[8,256,256]{2,1,0:T(8,128)(2,1)} %get-tuple-element.84.cotangent_ref) | copy-start | bytes 3145732 | tf_op jit(solution)/shard_map/cond
  102.2 103.7 %copy-start.5 = (bf16[128,256]{1,0:T(8,128)(2,1)S(1)}, bf16[128,256]{1,0:T(8,128)(2,1)}, u32[]{:S(2)}) copy-start(bf16[128,256]{1,0:T(8,128)(2,1)} %get-tuple-element.83.weight_ref) | copy-start | bytes 196612 | tf_op jit(solution)/shard_map/cond
  217.9 65.5 %all-to-all-start.8 = ((bf16[128,144,128]{2,1,0:T(8,128)(2,1)}), bf16[128,144,128]{2,1,0:T(8,128)(2,1)}, u32[]{:S(2)}, u32[]{:S(2)}) async-start(bf16[128,144,128]{2,1,0:T(8,128)(2,1)} %get-tuple-element.86), calls=%async_computation.8 | async-start | bytes 9437184 | tf_op jit(solution)/shard_map/cond/branch_1_fun/all_to_all | solution.py:313
  288.9 123.6 %all-to-all-start.9 = ((bf16[128,272,128]{2,1,0:T(8,128)(2,1)}), bf16[128,272,128]{2,1,0:T(8,128)(2,1)}, u32[]{:S(2)}, u32[]{:S(2)}) async-start(bf16[128,272,128]{2,1,0:T(8,128)(2,1)} %branch_1_fun.13), calls=%async_computation.9 | async-start | bytes 17825792 | tf_op jit(solution)/shard_map/cond/branch_1_fun/all_to_all | solution.py:313

commit v4 on v3

--- a/solution.py
+++ b/solution.py
@@ -335,7 +335,10 @@
     free_ref[...] = jnp.broadcast_to(free[:, None, :], free_ref.shape)
     route = jnp.where((named > 0) & (flipped > 0), OPEN, -1)
     spare = 1 - flipped.astype(jnp.int32)
-    at_ids = lax.broadcasted_iota(jnp.int32, (8, peers), 0)
+    needs = jnp.sum((route == OPEN).astype(jnp.float32), axis=1, keepdims=True).astype(jnp.int32)
+    ranks = (peers - needs) * 8 + (u_ids & 7)
+    ranks = [ranks[8 * group : 8 * group + 8] for group in range(groups)]
+    lowest = 16 * peers
     v_ids = lax.broadcasted_iota(jnp.int32, (8, peers), 1)
 
     def left_open(routes):
@@ -348,11 +351,11 @@
         shifts = [(turn + 8 * group) & (peers - 1) for group in range(groups)]
         rooms = [free_ref[shift] for shift in shifts]
         next_routes, next_spares, taken = [], [], []
-        for route, spare, shift, room in zip(routes, spares, shifts, rooms):
+        for route, spare, rank, shift, room in zip(routes, spares, ranks, shifts, rooms):
             fits = (route == OPEN) & ((spare & room) > 0)
-            first = jnp.min(jnp.where(fits, at_ids, 8), axis=0, keepdims=True)
-            chosen = fits & (at_ids == first)
-            taken.append(jnp.where(first < 8, 0, room))
+            first = jnp.min(jnp.where(fits, rank, lowest), axis=0, keepdims=True)
+            chosen = fits & (rank == first)
+            taken.append(jnp.where(first < lowest, 0, room))
             next_routes.append(jnp.where(chosen, (v_ids + shift) & (peers - 1), route))
             next_spares.append(pltpu.roll(jnp.where(chosen, 0, spare), peers - 1, 1))
         for shift, room in zip(shifts, taken):
@@ -667,7 +670,18 @@
     ]
 
 
-def late_sums(plan_ref, slots_ref, second_ref, tiles_ref, start_ref, total_ref, landed_ref, held_ref, sems):
+def late_sums(
+    plan_ref,
+    slots_ref,
+    second_ref,
+    tiles_ref,
+    start_ref,
+    total_ref,
+    landed_ref,
+    held_ref,
+    sems,
+    landed=None,
+):
     peers = plan_ref.shape[1]
     slot_total, rows, half = held_ref.shape
     locals_ = start_ref.shape[0]
@@ -710,6 +724,9 @@
     for part in range(PARTS):
         landing(part).wait()
         lax.fori_loop(part * share, (part + 1) * share, add, 0, unroll=4)
+
+    if landed is not None:
+        landed()
 
     def multiply(group, carry):
         @pl.when(group <= slots_ref[LAST, 0])
@@ -871,6 +888,16 @@
     late_sems,
     rows_ref,
 ):
+    rows = held_ref.shape[1]
+    width = out_ref.shape[2]
+
+    def put_rows_together():
+        rows_ref[...] = landed_ref[:, pl.ds(rows, EXTRA)].astype(jnp.float32)
+        for side in range(2):
+            weight_grad_ref[:, side * width : (side + 1) * width] = (
+                rows_ref[:, 4 + side, :] + rows_ref[:, 2 + side, :] + rows_ref[:, side, :]
+            ) * scale
+
     late_sums(
         plan_ref,
         slots_ref,
@@ -881,15 +908,9 @@
         landed_ref,
         held_ref,
         late_sems,
+        put_rows_together,
     )
-    rows = held_ref.shape[1]
-    width = out_ref.shape[2]
     out_ref[...] = total_ref[pl.ds(0, out_ref.shape[0])].astype(out_ref.dtype)
-    rows_ref[...] = landed_ref[:, pl.ds(rows, EXTRA)].astype(jnp.float32)
-    for side in range(2):
-        weight_grad_ref[:, side * width : (side + 1) * width] = (
-            rows_ref[:, 4 + side, :] + rows_ref[:, 2 + side, :] + rows_ref[:, side, :]
-        ) * scale
 
 
 def last(plan, slots, second, tile_values, start, scale):

time: 423 us -> 422 us (level)
  waiting for transfers between devices: 253 us -> 265 us
  Pallas kernels: 115 us -> 104 us
    all_to_all x5, waiting for transfers between devices: 253 us -> 265 us  [exchange(): lax.all_to_all(values, 'nodes', split_axis=0, concat_axis=0, tiled=True)]
    pallas_call x2, Pallas kernels: 58.8 us -> 49.7 us  [own_products(): pl.pallas_call(products_kernel, grid_spec=pltpu.PrefetchScalarGridSpec(nu...]
  transfers between devices with their start and end apart: 5 -> 5, of which waited for: 5 -> 5; matrix products, arithmetic and copies ran while one was open for 0% -> 0% of each run, Pallas kernels for 18% -> 15%
where the time goes in v4:
time: 422 us; the launch traced here: 421 us
  waiting for transfers between devices  265 us (63%)
  Pallas kernels  104 us (25%)
  starting transfers between devices  44.7 us (11%)
    all_to_all x5, waiting for transfers between devices, exchange(): lax.all_to_all(values, 'nodes', split_axis=0, concat_axis=0, tiled=True)  265 us
    pallas_call x2, Pallas kernels, own_products(): pl.pallas_call(products_kernel, grid_spec=pltpu.PrefetchScalarGridSpec(nu...  49.7 us
    all_to_all x5, starting transfers between devices, exchange(): lax.all_to_all(values, 'nodes', split_axis=0, concat_axis=0, tiled=True)  44.7 us
    pallas_call x2, Pallas kernels, early_products(): pl.pallas_call(early_kernel, grid_spec=pltpu.PrefetchScalarGridSpec(num_s...  15.2 us
    pallas_call x1, Pallas kernels, layer(): pl.pallas_call(layer_kernel, grid_spec=pltpu.PrefetchScalarGridSpec(num_s...  11.5 us
    pallas_call x2, Pallas kernels, relay(): pl.pallas_call(relay_kernel, grid_spec=pltpu.PrefetchScalarGridSpec(num_s...  10.9 us
  transfers between devices with their start and end apart: 5, of which 5 were waited for; matrix products, arithmetic and copies ran while one was open for 0% of the time, Pallas kernels for 15%

profile of v4, /device:TPU:38, one launch (start us, length us, event | category | flops | bytes accessed | tf_op | source)
XLA Modules:
  0.0 421.3 jit_solution(7610018236326848352)
XLA Ops:
  1.3 0.7 and_select_fusion.2
  2.0 0.7 compare_and_fusion
  2.8 0.7 broadcast_in_dim.68
  3.5 10.2 %all-to-all-start.10 = ((s32[128,1,128]{2,1,0:T(1,128)}), s32[128,1,128]{2,1,0:T(1,128)S(1)}, u32[]{:S(2)}, u32[]{:S(2)}) async-start(s32[128,1,128]{2,1,0:T(1,128)} %broadcast_in_dim.68), calls=%async_computation.10 | async-start | bytes 131072 | tf_op jit(solution)/shard_map/all_to_all | solution.py:313
  13.7 0.7 clamp_bitcast_fusion
  14.4 6.3 %all-to-all-done.10 = s32[128,1,128]{2,1,0:T(1,128)S(1)} async-done(((s32[128,1,128]{2,1,0:T(1,128)}), s32[128,1,128]{2,1,0:T(1,128)S(1)}, u32[]{:S(2)}, u32[]{:S(2)}) %all-to-all-start.10) | async-done | bytes 65568 | tf_op jit(solution)/shard_map/all_to_all | solution.py:313
  21.2 8.3 %shard_map.85 = (s32[8,128]{1,0:T(8,128)S(1)}, bf16[128,128,128]{2,1,0:T(8,128)(2,1)}) custom-call(s32[1]{0:T(128)} %bitcast.7.me_ref, s32[128,128]{1,0:T(8,128)} %bitcast.44, bf16[8,256,128]{2,1,0:T(8,128)(2,1)} %bitcast.37), custom_call_target="tpu_custom_call" | custom-call | tf_op jit(solution)/shard_map/pallas_call | solution.py:414
  30.7 390.4 %conditional.1 = (bf16[8,256,256]{2,1,0:T(8,128)(2,1)}, f32[128,256]{1,0:T(8,128)}, bf16[2048,128]{1,0:T(8,128)(2,1)}) conditional(s32[]{:T(128)} %bitcast.12, (s32[8,128]{1,0:T(8,128)S(1)}, s32[96]{0:T(128)S(1)}, pred[96]{0:T(512)(128)(4,1)S(1)}, s32[96]{0:T(128)S(1)}, pred[96]{0:T(512)(128)(4,1)S(1)}, /*index=5*/s32[96]{0:T(128)S(1)}, ...), branch_computations={%region_2.5_spmd, %region_5.6_spmd} | conditional | flops 8053135360 | bytes 209198976 | solution.py:1011
  30.8 8.4 %all-to-all-start.6 = ((bf16[128,128,128]{2,1,0:T(8,128)(2,1)}), bf16[128,128,128]{2,1,0:T(8,128)(2,1)}, u32[]{:S(2)}, u32[]{:S(2)}) async-start(bf16[128,128,128]{2,1,0:T(8,128)(2,1)} %get-tuple-element.76), calls=%async_computation.6 | async-start | bytes 8388608 | tf_op jit(solution)/shard_map/cond/branch_1_fun/all_to_all | solution.py:313
  40.6 24.8 %branch_1_fun.8 = (bf16[128,256,128]{2,1,0:T(8,128)(2,1)}, f32[8,256,128]{2,1,0:T(8,128)}) custom-call(s32[8,128]{1,0:T(8,128)S(1)} %get-tuple-element.68.plan_ref, s32[4,96]{1,0:T(4,128)} %add_add_fusion.slots_ref, bf16[8,256,128]{2,1,0:T(8,128)(2,1)S(1)} %copy-done.1, bf16[96,256,256]{2,1,0:T(8,128)(2,1)} %get-tuple-element.78.tiles_ref), custom_call_target="tpu_custom_call" | custom-call | flops 2415919104 | bytes 25165824 | tf_op jit(solution)/shard_map/cond/branch_1_fun/pallas_call | solution.py:512
  65.4 24.1 %all-to-all-done.6.came_ref.first_ref = bf16[128,128,128]{2,1,0:T(8,128)(2,1)} async-done(((bf16[128,128,128]{2,1,0:T(8,128)(2,1)}), bf16[128,128,128]{2,1,0:T(8,128)(2,1)}, u32[]{:S(2)}, u32[]{:S(2)}) %all-to-all-start.6) | async-done | bytes 4194336 | tf_op jit(solution)/shard_map/cond/branch_1_fun/all_to_all | solution.py:313
  89.4 5.1 %branch_1_fun.9 = bf16[128,256,128]{2,1,0:T(8,128)(2,1)} custom-call(s32[8,128]{1,0:T(8,128)S(1)} %get-tuple-element.68.plan_ref, bf16[128,128,128]{2,1,0:T(8,128)(2,1)} %all-to-all-done.6.came_ref.first_ref, bf16[128,256,128]{2,1,0:T(8,128)(2,1)} %get-tuple-element.81._), custom_call_target="tpu_custom_call", output_to_operand_aliasing={{}: (2, {})} | custom-call | tf_op jit(solution)/shard_map/cond/branch_1_fun/pallas_call | solution.py:594
  94.6 8.4 %all-to-all-start.7 = ((bf16[128,256,128]{2,1,0:T(8,128)(2,1)}), bf16[128,256,128]{2,1,0:T(8,128)(2,1)}, u32[]{:S(2)}, u32[]{:S(2)}) async-start(bf16[128,256,128]{2,1,0:T(8,128)(2,1)} %branch_1_fun.9), calls=%async_computation.7 | async-start | bytes 16777216 | tf_op jit(solution)/shard_map/cond/branch_1_fun/all_to_all | solution.py:313
  103.1 7.6 %branch_1_fun.10.start_ref = f32[8,256,128]{2,1,0:T(8,128)} custom-call(s32[8,128]{1,0:T(8,128)S(1)} %get-tuple-element.68.plan_ref, s32[4,96]{1,0:T(4,128)} %add_add_fusion.slots_ref, bf16[128,128,128]{2,1,0:T(8,128)(2,1)} %all-to-all-done.6.came_ref.first_ref, bf16[96,256,256]{2,1,0:T(8,128)(2,1)} %get-tuple-element.78.tiles_ref, ...), custom_call_target="tpu_custom_call" | custom-call | flops 805306368 | bytes 12582912 | tf_op jit(solution)/shard_map/cond/branch_1_fun/pallas_call | solution.py:638
  110.7 96.1 %all-to-all-done.7.second_ref = bf16[128,256,128]{2,1,0:T(8,128)(2,1)} async-done(((bf16[128,256,128]{2,1,0:T(8,128)(2,1)}), bf16[128,256,128]{2,1,0:T(8,128)(2,1)}, u32[]{:S(2)}, u32[]{:S(2)}) %all-to-all-start.7) | async-done | bytes 8388640 | tf_op jit(solution)/shard_map/cond/branch_1_fun/all_to_all | solution.py:313
  206.8 11.5 %branch_1_fun.11 = (bf16[8,256,256]{2,1,0:T(8,128)(2,1)}, bf16[8,256,128]{2,1,0:T(8,128)(2,1)}, bf16[128,144,128]{2,1,0:T(8,128)(2,1)}) custom-call(s32[8,128]{1,0:T(8,128)S(1)} %get-tuple-element.68.plan_ref, s32[4,96]{1,0:T(4,128)} %add_add_fusion.slots_ref, bf16[128,256,128]{2,1,0:T(8,128)(2,1)} %all-to-all-done.7.second_ref, ...), custom_call_target="tpu_custom_call" | custom-call | tf_op jit(solution)/shard_map/cond/branch_1_fun/pallas_call | solution.py:849
  218.3 9.0 %all-to-all-start.8 = ((bf16[128,144,128]{2,1,0:T(8,128)(2,1)}), bf16[128,144,128]{2,1,0:T(8,128)(2,1)}, u32[]{:S(2)}, u32[]{:S(2)}) async-start(bf16[128,144,128]{2,1,0:T(8,128)(2,1)} %get-tuple-element.86), calls=%async_computation.8 | async-start | bytes 9437184 | tf_op jit(solution)/shard_map/cond/branch_1_fun/all_to_all | solution.py:313
  227.3 24.9 %branch_1_fun.12 = (bf16[128,272,128]{2,1,0:T(8,128)(2,1)}, f32[8,256,128]{2,1,0:T(8,128)}) custom-call(s32[8,128]{1,0:T(8,128)S(1)} %get-tuple-element.68.plan_ref, s32[4,96]{1,0:T(4,128)} %add_add_fusion.slots_ref, bf16[8,256,128]{2,1,0:T(8,128)(2,1)} %get-tuple-element.87.blocks_ref, bf16[96,256,256]{2,1,0:T(8,128)(2,1)} %get-tuple-element.78.tiles_ref), custom_call_target="tpu_custom_call" | custom-call | flops 2415919104 | bytes 25165824 | tf_op jit(solution)/shard_map/cond/branch_1_fun/pallas_call | solution.py:512
  252.2 31.3 %all-to-all-done.8.came_ref.first_ref = bf16[128,144,128]{2,1,0:T(8,128)(2,1)} async-done(((bf16[128,144,128]{2,1,0:T(8,128)(2,1)}), bf16[128,144,128]{2,1,0:T(8,128)(2,1)}, u32[]{:S(2)}, u32[]{:S(2)}) %all-to-all-start.8) | async-done | bytes 4718624 | tf_op jit(solution)/shard_map/cond/branch_1_fun/all_to_all | solution.py:313
  283.5 5.8 %branch_1_fun.13 = bf16[128,272,128]{2,1,0:T(8,128)(2,1)} custom-call(s32[8,128]{1,0:T(8,128)S(1)} %get-tuple-element.68.plan_ref, bf16[128,144,128]{2,1,0:T(8,128)(2,1)} %all-to-all-done.8.came_ref.first_ref, bf16[128,272,128]{2,1,0:T(8,128)(2,1)} %get-tuple-element.90._), custom_call_target="tpu_custom_call", output_to_operand_aliasing={{}: (2, {})} | custom-call | tf_op jit(solution)/shard_map/cond/branch_1_fun/pallas_call | solution.py:594
  289.3 8.7 %all-to-all-start.9 = ((bf16[128,272,128]{2,1,0:T(8,128)(2,1)}), bf16[128,272,128]{2,1,0:T(8,128)(2,1)}, u32[]{:S(2)}, u32[]{:S(2)}) async-start(bf16[128,272,128]{2,1,0:T(8,128)(2,1)} %branch_1_fun.13), calls=%async_computation.9 | async-start | bytes 17825792 | tf_op jit(solution)/shard_map/cond/branch_1_fun/all_to_all | solution.py:313
  298.0 7.6 %branch_1_fun.14.start_ref = f32[8,256,128]{2,1,0:T(8,128)} custom-call(s32[8,128]{1,0:T(8,128)S(1)} %get-tuple-element.68.plan_ref, s32[4,96]{1,0:T(4,128)} %add_add_fusion.slots_ref, bf16[128,144,128]{2,1,0:T(8,128)(2,1)} %all-to-all-done.8.came_ref.first_ref, bf16[96,256,256]{2,1,0:T(8,128)(2,1)} %get-tuple-element.78.tiles_ref, ...), custom_call_target="tpu_custom_call" | custom-call | flops 805306368 | bytes 12582912 | tf_op jit(solution)/shard_map/cond/branch_1_fun/pallas_call | solution.py:638
  305.6 107.0 %all-to-all-done.9.second_ref = bf16[128,272,128]{2,1,0:T(8,128)(2,1)} async-done(((bf16[128,272,128]{2,1,0:T(8,128)(2,1)}), bf16[128,272,128]{2,1,0:T(8,128)(2,1)}, u32[]{:S(2)}, u32[]{:S(2)}) %all-to-all-start.9) | async-done | bytes 8912928 | tf_op jit(solution)/shard_map/cond/branch_1_fun/all_to_all | solution.py:313
  412.7 8.2 %branch_1_fun.15 = (bf16[8,256,128]{2,1,0:T(8,128)(2,1)}, f32[128,256]{1,0:T(8,128)}) custom-call(s32[8,128]{1,0:T(8,128)S(1)} %get-tuple-element.68.plan_ref, s32[4,96]{1,0:T(4,128)} %add_add_fusion.slots_ref, bf16[128,272,128]{2,1,0:T(8,128)(2,1)} %all-to-all-done.9.second_ref, bf16[96,256,256]{2,1,0:T(8,128)(2,1)} %get-tuple-element.78.tiles_ref, ...), custom_call_target="tpu_custom_call" | custom-call | tf_op jit(solution)/shard_map/cond/branch_1_fun/pallas_call | solution.py:921
  (15 shorter events, 2.0 us)
Async XLA Ops:
  3.5 17.1 %all-to-all-start.10 = ((s32[128,1,128]{2,1,0:T(1,128)}), s32[128,1,128]{2,1,0:T(1,128)S(1)}, u32[]{:S(2)}, u32[]{:S(2)}) async-start(s32[128,1,128]{2,1,0:T(1,128)} %broadcast_in_dim.68), calls=%async_computation.10 | async-start | bytes 131072 | tf_op jit(solution)/shard_map/all_to_all | solution.py:313
  20.6 0.6 copy-start.6
  30.7 9.8 %copy-start.1 = (bf16[8,256,128]{2,1,0:T(8,128)(2,1)S(1)}, bf16[8,256,128]{2,1,0:T(8,128)(2,1)}, u32[]{:S(2)}) copy-start(bf16[8,256,128]{2,1,0:T(8,128)(2,1)} %get-tuple-element.77.blocks_ref) | copy-start | bytes 1572868 | tf_op jit(solution)/shard_map/cond
  30.8 58.7 %all-to-all-start.6 = ((bf16[128,128,128]{2,1,0:T(8,128)(2,1)}), bf16[128,128,128]{2,1,0:T(8,128)(2,1)}, u32[]{:S(2)}, u32[]{:S(2)}) async-start(bf16[128,128,128]{2,1,0:T(8,128)(2,1)} %get-tuple-element.76), calls=%async_computation.6 | async-start | bytes 8388608 | tf_op jit(solution)/shard_map/cond/branch_1_fun/all_to_all | solution.py:313
  94.6 112.2 %all-to-all-start.7 = ((bf16[128,256,128]{2,1,0:T(8,128)(2,1)}), bf16[128,256,128]{2,1,0:T(8,128)(2,1)}, u32[]{:S(2)}, u32[]{:S(2)}) async-start(bf16[128,256,128]{2,1,0:T(8,128)(2,1)} %branch_1_fun.9), calls=%async_computation.7 | async-start | bytes 16777216 | tf_op jit(solution)/shard_map/cond/branch_1_fun/all_to_all | solution.py:313
  103.0 103.7 %copy-start.3 = (bf16[8,256,256]{2,1,0:T(8,128)(2,1)S(1)}, bf16[8,256,256]{2,1,0:T(8,128)(2,1)}, u32[]{:S(2)}) copy-start(bf16[8,256,256]{2,1,0:T(8,128)(2,1)} %get-tuple-element.84.cotangent_ref) | copy-start | bytes 3145732 | tf_op jit(solution)/shard_map/cond
  103.0 103.7 %copy-start.5 = (bf16[128,256]{1,0:T(8,128)(2,1)S(1)}, bf16[128,256]{1,0:T(8,128)(2,1)}, u32[]{:S(2)}) copy-start(bf16[128,256]{1,0:T(8,128)(2,1)} %get-tuple-element.83.weight_ref) | copy-start | bytes 196612 | tf_op jit(solution)/shard_map/cond
  218.3 65.2 %all-to-all-start.8 = ((bf16[128,144,128]{2,1,0:T(8,128)(2,1)}), bf16[128,144,128]{2,1,0:T(8,128)(2,1)}, u32[]{:S(2)}, u32[]{:S(2)}) async-start(bf16[128,144,128]{2,1,0:T(8,128)(2,1)} %get-tuple-element.86), calls=%async_computation.8 | async-start | bytes 9437184 | tf_op jit(solution)/shard_map/cond/branch_1_fun/all_to_all | solution.py:313
  289.3 123.4 %all-to-all-start.9 = ((bf16[128,272,128]{2,1,0:T(8,128)(2,1)}), bf16[128,272,128]{2,1,0:T(8,128)(2,1)}, u32[]{:S(2)}, u32[]{:S(2)}) async-start(bf16[128,272,128]{2,1,0:T(8,128)(2,1)} %branch_1_fun.13), calls=%async_computation.9 | async-start | bytes 17825792 | tf_op jit(solution)/shard_map/cond/branch_1_fun/all_to_all | solution.py:313

commit v5 on v4

--- a/solution.py
+++ b/solution.py
@@ -438,7 +438,7 @@
         act(q)
         return carry
 
-    lax.fori_loop(0, peers, step, 0, unroll=8)
+    lax.fori_loop(0, peers, step, 0, unroll=32)
 
 
 def start_first(plan_ref, blocks_ref, out_ref, sem):
@@ -723,7 +723,7 @@
 
     for part in range(PARTS):
         landing(part).wait()
-        lax.fori_loop(part * share, (part + 1) * share, add, 0, unroll=4)
+        lax.fori_loop(part * share, (part + 1) * share, add, 0, unroll=8)
 
     if landed is not None:
         landed()
@@ -819,7 +819,7 @@
             copy.start()
         return carry
 
-    lax.fori_loop(0, locals_, block_step, 0, unroll=2)
+    lax.fori_loop(0, locals_, block_step, 0, unroll=4)
     start_first(plan_ref, back_ref, out_ref, sems.at[2 * locals_ + 1])
     for side in range(2):
         parts = three_parts(grad_ref[:, side * width : (side + 1) * width])

time: 422 us -> 422 us (level)
  transfers between devices with their start and end apart: 5 -> 5, of which waited for: 5 -> 5; matrix products, arithmetic and copies ran while one was open for 0% -> 0% of each run, Pallas kernels for 15% -> 16%
where the time goes in v5:
time: 422 us; the launch traced here: 421 us
  waiting for transfers between devices  264 us (63%)
  Pallas kernels  103 us (24%)
  starting transfers between devices  45.7 us (11%)
    all_to_all x5, waiting for transfers between devices, exchange(): lax.all_to_all(values, 'nodes', split_axis=0, concat_axis=0, tiled=True)  264 us
    pallas_call x2, Pallas kernels, own_products(): pl.pallas_call(products_kernel, grid_spec=pltpu.PrefetchScalarGridSpec(nu...  50.4 us
    all_to_all x5, starting transfers between devices, exchange(): lax.all_to_all(values, 'nodes', split_axis=0, concat_axis=0, tiled=True)  45.7 us
    pallas_call x2, Pallas kernels, early_products(): pl.pallas_call(early_kernel, grid_spec=pltpu.PrefetchScalarGridSpec(num_s...  15.2 us
    pallas_call x1, Pallas kernels, layer(): pl.pallas_call(layer_kernel, grid_spec=pltpu.PrefetchScalarGridSpec(num_s...  11.3 us
    pallas_call x2, Pallas kernels, relay(): pl.pallas_call(relay_kernel, grid_spec=pltpu.PrefetchScalarGridSpec(num_s...  10.6 us
  transfers between devices with their start and end apart: 5, of which 5 were waited for; matrix products, arithmetic and copies ran while one was open for 0% of the time, Pallas kernels for 16%

profile of v5, /device:TPU:38, one launch (start us, length us, event | category | flops | bytes accessed | tf_op | source)
XLA Modules:
  0.0 421.0 jit_solution(10545431708247861933)
XLA Ops:
  1.3 0.7 and_select_fusion.2
  2.0 0.7 compare_and_fusion
  2.8 0.7 broadcast_in_dim.68
  3.5 10.2 %all-to-all-start.10 = ((s32[128,1,128]{2,1,0:T(1,128)}), s32[128,1,128]{2,1,0:T(1,128)S(1)}, u32[]{:S(2)}, u32[]{:S(2)}) async-start(s32[128,1,128]{2,1,0:T(1,128)} %broadcast_in_dim.68), calls=%async_computation.10 | async-start | bytes 131072 | tf_op jit(solution)/shard_map/all_to_all | solution.py:313
  13.7 0.7 clamp_bitcast_fusion
  14.4 6.3 %all-to-all-done.10 = s32[128,1,128]{2,1,0:T(1,128)S(1)} async-done(((s32[128,1,128]{2,1,0:T(1,128)}), s32[128,1,128]{2,1,0:T(1,128)S(1)}, u32[]{:S(2)}, u32[]{:S(2)}) %all-to-all-start.10) | async-done | bytes 65568 | tf_op jit(solution)/shard_map/all_to_all | solution.py:313
  21.2 7.6 %shard_map.85 = (s32[8,128]{1,0:T(8,128)S(1)}, bf16[128,128,128]{2,1,0:T(8,128)(2,1)}) custom-call(s32[1]{0:T(128)} %bitcast.7.me_ref, s32[128,128]{1,0:T(8,128)} %bitcast.44, bf16[8,256,128]{2,1,0:T(8,128)(2,1)} %bitcast.37), custom_call_target="tpu_custom_call" | custom-call | tf_op jit(solution)/shard_map/pallas_call | solution.py:414
  30.0 390.8 %conditional.1 = (bf16[8,256,256]{2,1,0:T(8,128)(2,1)}, f32[128,256]{1,0:T(8,128)}, bf16[2048,128]{1,0:T(8,128)(2,1)}) conditional(s32[]{:T(128)} %bitcast.12, (s32[8,128]{1,0:T(8,128)S(1)}, s32[96]{0:T(128)S(1)}, pred[96]{0:T(512)(128)(4,1)S(1)}, s32[96]{0:T(128)S(1)}, pred[96]{0:T(512)(128)(4,1)S(1)}, /*index=5*/s32[96]{0:T(128)S(1)}, ...), branch_computations={%region_2.5_spmd, %region_5.6_spmd} | conditional | flops 8053135360 | bytes 209198976 | solution.py:1011
  30.0 8.4 %all-to-all-start.6 = ((bf16[128,128,128]{2,1,0:T(8,128)(2,1)}), bf16[128,128,128]{2,1,0:T(8,128)(2,1)}, u32[]{:S(2)}, u32[]{:S(2)}) async-start(bf16[128,128,128]{2,1,0:T(8,128)(2,1)} %get-tuple-element.76), calls=%async_computation.6 | async-start | bytes 8388608 | tf_op jit(solution)/shard_map/cond/branch_1_fun/all_to_all | solution.py:313
  39.8 25.1 %branch_1_fun.8 = (bf16[128,256,128]{2,1,0:T(8,128)(2,1)}, f32[8,256,128]{2,1,0:T(8,128)}) custom-call(s32[8,128]{1,0:T(8,128)S(1)} %get-tuple-element.68.plan_ref, s32[4,96]{1,0:T(4,128)} %add_add_fusion.slots_ref, bf16[8,256,128]{2,1,0:T(8,128)(2,1)S(1)} %copy-done.1, bf16[96,256,256]{2,1,0:T(8,128)(2,1)} %get-tuple-element.78.tiles_ref), custom_call_target="tpu_custom_call" | custom-call | flops 2415919104 | bytes 25165824 | tf_op jit(solution)/shard_map/cond/branch_1_fun/pallas_call | solution.py:512
  65.0 23.7 %all-to-all-done.6.came_ref.first_ref = bf16[128,128,128]{2,1,0:T(8,128)(2,1)} async-done(((bf16[128,128,128]{2,1,0:T(8,128)(2,1)}), bf16[128,128,128]{2,1,0:T(8,128)(2,1)}, u32[]{:S(2)}, u32[]{:S(2)}) %all-to-all-start.6) | async-done | bytes 4194336 | tf_op jit(solution)/shard_map/cond/branch_1_fun/all_to_all | solution.py:313
  88.7 5.0 %branch_1_fun.9 = bf16[128,256,128]{2,1,0:T(8,128)(2,1)} custom-call(s32[8,128]{1,0:T(8,128)S(1)} %get-tuple-element.68.plan_ref, bf16[128,128,128]{2,1,0:T(8,128)(2,1)} %all-to-all-done.6.came_ref.first_ref, bf16[128,256,128]{2,1,0:T(8,128)(2,1)} %get-tuple-element.81._), custom_call_target="tpu_custom_call", output_to_operand_aliasing={{}: (2, {})} | custom-call | tf_op jit(solution)/shard_map/cond/branch_1_fun/pallas_call | solution.py:594
  93.7 8.4 %all-to-all-start.7 = ((bf16[128,256,128]{2,1,0:T(8,128)(2,1)}), bf16[128,256,128]{2,1,0:T(8,128)(2,1)}, u32[]{:S(2)}, u32[]{:S(2)}) async-start(bf16[128,256,128]{2,1,0:T(8,128)(2,1)} %branch_1_fun.9), calls=%async_computation.7 | async-start | bytes 16777216 | tf_op jit(solution)/shard_map/cond/branch_1_fun/all_to_all | solution.py:313
  102.2 7.6 %branch_1_fun.10.start_ref = f32[8,256,128]{2,1,0:T(8,128)} custom-call(s32[8,128]{1,0:T(8,128)S(1)} %get-tuple-element.68.plan_ref, s32[4,96]{1,0:T(4,128)} %add_add_fusion.slots_ref, bf16[128,128,128]{2,1,0:T(8,128)(2,1)} %all-to-all-done.6.came_ref.first_ref, bf16[96,256,256]{2,1,0:T(8,128)(2,1)} %get-tuple-element.78.tiles_ref, ...), custom_call_target="tpu_custom_call" | custom-call | flops 805306368 | bytes 12582912 | tf_op jit(solution)/shard_map/cond/branch_1_fun/pallas_call | solution.py:638
  109.8 96.1 %all-to-all-done.7.second_ref = bf16[128,256,128]{2,1,0:T(8,128)(2,1)} async-done(((bf16[128,256,128]{2,1,0:T(8,128)(2,1)}), bf16[128,256,128]{2,1,0:T(8,128)(2,1)}, u32[]{:S(2)}, u32[]{:S(2)}) %all-to-all-start.7) | async-done | bytes 8388640 | tf_op jit(solution)/shard_map/cond/branch_1_fun/all_to_all | solution.py:313
  205.9 11.3 %branch_1_fun.11 = (bf16[8,256,256]{2,1,0:T(8,128)(2,1)}, bf16[8,256,128]{2,1,0:T(8,128)(2,1)}, bf16[128,144,128]{2,1,0:T(8,128)(2,1)}) custom-call(s32[8,128]{1,0:T(8,128)S(1)} %get-tuple-element.68.plan_ref, s32[4,96]{1,0:T(4,128)} %add_add_fusion.slots_ref, bf16[128,256,128]{2,1,0:T(8,128)(2,1)} %all-to-all-done.7.second_ref, ...), custom_call_target="tpu_custom_call" | custom-call | tf_op jit(solution)/shard_map/cond/branch_1_fun/pallas_call | solution.py:849
  217.2 9.9 %all-to-all-start.8 = ((bf16[128,144,128]{2,1,0:T(8,128)(2,1)}), bf16[128,144,128]{2,1,0:T(8,128)(2,1)}, u32[]{:S(2)}, u32[]{:S(2)}) async-start(bf16[128,144,128]{2,1,0:T(8,128)(2,1)} %get-tuple-element.86), calls=%async_computation.8 | async-start | bytes 9437184 | tf_op jit(solution)/shard_map/cond/branch_1_fun/all_to_all | solution.py:313
  227.1 25.3 %branch_1_fun.12 = (bf16[128,272,128]{2,1,0:T(8,128)(2,1)}, f32[8,256,128]{2,1,0:T(8,128)}) custom-call(s32[8,128]{1,0:T(8,128)S(1)} %get-tuple-element.68.plan_ref, s32[4,96]{1,0:T(4,128)} %add_add_fusion.slots_ref, bf16[8,256,128]{2,1,0:T(8,128)(2,1)} %get-tuple-element.87.blocks_ref, bf16[96,256,256]{2,1,0:T(8,128)(2,1)} %get-tuple-element.78.tiles_ref), custom_call_target="tpu_custom_call" | custom-call | flops 2415919104 | bytes 25165824 | tf_op jit(solution)/shard_map/cond/branch_1_fun/pallas_call | solution.py:512
  252.4 31.0 %all-to-all-done.8.came_ref.first_ref = bf16[128,144,128]{2,1,0:T(8,128)(2,1)} async-done(((bf16[128,144,128]{2,1,0:T(8,128)(2,1)}), bf16[128,144,128]{2,1,0:T(8,128)(2,1)}, u32[]{:S(2)}, u32[]{:S(2)}) %all-to-all-start.8) | async-done | bytes 4718624 | tf_op jit(solution)/shard_map/cond/branch_1_fun/all_to_all | solution.py:313
  283.4 5.6 %branch_1_fun.13 = bf16[128,272,128]{2,1,0:T(8,128)(2,1)} custom-call(s32[8,128]{1,0:T(8,128)S(1)} %get-tuple-element.68.plan_ref, bf16[128,144,128]{2,1,0:T(8,128)(2,1)} %all-to-all-done.8.came_ref.first_ref, bf16[128,272,128]{2,1,0:T(8,128)(2,1)} %get-tuple-element.90._), custom_call_target="tpu_custom_call", output_to_operand_aliasing={{}: (2, {})} | custom-call | tf_op jit(solution)/shard_map/cond/branch_1_fun/pallas_call | solution.py:594
  288.9 8.8 %all-to-all-start.9 = ((bf16[128,272,128]{2,1,0:T(8,128)(2,1)}), bf16[128,272,128]{2,1,0:T(8,128)(2,1)}, u32[]{:S(2)}, u32[]{:S(2)}) async-start(bf16[128,272,128]{2,1,0:T(8,128)(2,1)} %branch_1_fun.13), calls=%async_computation.9 | async-start | bytes 17825792 | tf_op jit(solution)/shard_map/cond/branch_1_fun/all_to_all | solution.py:313
  297.7 7.6 %branch_1_fun.14.start_ref = f32[8,256,128]{2,1,0:T(8,128)} custom-call(s32[8,128]{1,0:T(8,128)S(1)} %get-tuple-element.68.plan_ref, s32[4,96]{1,0:T(4,128)} %add_add_fusion.slots_ref, bf16[128,144,128]{2,1,0:T(8,128)(2,1)} %all-to-all-done.8.came_ref.first_ref, bf16[96,256,256]{2,1,0:T(8,128)(2,1)} %get-tuple-element.78.tiles_ref, ...), custom_call_target="tpu_custom_call" | custom-call | flops 805306368 | bytes 12582912 | tf_op jit(solution)/shard_map/cond/branch_1_fun/pallas_call | solution.py:638
  305.4 107.0 %all-to-all-done.9.second_ref = bf16[128,272,128]{2,1,0:T(8,128)(2,1)} async-done(((bf16[128,272,128]{2,1,0:T(8,128)(2,1)}), bf16[128,272,128]{2,1,0:T(8,128)(2,1)}, u32[]{:S(2)}, u32[]{:S(2)}) %all-to-all-start.9) | async-done | bytes 8912928 | tf_op jit(solution)/shard_map/cond/branch_1_fun/all_to_all | solution.py:313
  412.4 8.2 %branch_1_fun.15 = (bf16[8,256,128]{2,1,0:T(8,128)(2,1)}, f32[128,256]{1,0:T(8,128)}) custom-call(s32[8,128]{1,0:T(8,128)S(1)} %get-tuple-element.68.plan_ref, s32[4,96]{1,0:T(4,128)} %add_add_fusion.slots_ref, bf16[128,272,128]{2,1,0:T(8,128)(2,1)} %all-to-all-done.9.second_ref, bf16[96,256,256]{2,1,0:T(8,128)(2,1)} %get-tuple-element.78.tiles_ref, ...), custom_call_target="tpu_custom_call" | custom-call | tf_op jit(solution)/shard_map/cond/branch_1_fun/pallas_call | solution.py:921
  (15 shorter events, 2.0 us)
Async XLA Ops:
  3.5 17.1 %all-to-all-start.10 = ((s32[128,1,128]{2,1,0:T(1,128)}), s32[128,1,128]{2,1,0:T(1,128)S(1)}, u32[]{:S(2)}, u32[]{:S(2)}) async-start(s32[128,1,128]{2,1,0:T(1,128)} %broadcast_in_dim.68), calls=%async_computation.10 | async-start | bytes 131072 | tf_op jit(solution)/shard_map/all_to_all | solution.py:313
  20.6 0.6 copy-start.6
  30.0 9.8 %copy-start.1 = (bf16[8,256,128]{2,1,0:T(8,128)(2,1)S(1)}, bf16[8,256,128]{2,1,0:T(8,128)(2,1)}, u32[]{:S(2)}) copy-start(bf16[8,256,128]{2,1,0:T(8,128)(2,1)} %get-tuple-element.77.blocks_ref) | copy-start | bytes 1572868 | tf_op jit(solution)/shard_map/cond
  30.0 58.7 %all-to-all-start.6 = ((bf16[128,128,128]{2,1,0:T(8,128)(2,1)}), bf16[128,128,128]{2,1,0:T(8,128)(2,1)}, u32[]{:S(2)}, u32[]{:S(2)}) async-start(bf16[128,128,128]{2,1,0:T(8,128)(2,1)} %get-tuple-element.76), calls=%async_computation.6 | async-start | bytes 8388608 | tf_op jit(solution)/shard_map/cond/branch_1_fun/all_to_all | solution.py:313
  93.7 112.2 %all-to-all-start.7 = ((bf16[128,256,128]{2,1,0:T(8,128)(2,1)}), bf16[128,256,128]{2,1,0:T(8,128)(2,1)}, u32[]{:S(2)}, u32[]{:S(2)}) async-start(bf16[128,256,128]{2,1,0:T(8,128)(2,1)} %branch_1_fun.9), calls=%async_computation.7 | async-start | bytes 16777216 | tf_op jit(solution)/shard_map/cond/branch_1_fun/all_to_all | solution.py:313
  102.2 103.8 %copy-start.3 = (bf16[8,256,256]{2,1,0:T(8,128)(2,1)S(1)}, bf16[8,256,256]{2,1,0:T(8,128)(2,1)}, u32[]{:S(2)}) copy-start(bf16[8,256,256]{2,1,0:T(8,128)(2,1)} %get-tuple-element.84.cotangent_ref) | copy-start | bytes 3145732 | tf_op jit(solution)/shard_map/cond
  102.2 103.8 %copy-start.5 = (bf16[128,256]{1,0:T(8,128)(2,1)S(1)}, bf16[128,256]{1,0:T(8,128)(2,1)}, u32[]{:S(2)}) copy-start(bf16[128,256]{1,0:T(8,128)(2,1)} %get-tuple-element.83.weight_ref) | copy-start | bytes 196612 | tf_op jit(solution)/shard_map/cond
  217.2 66.1 %all-to-all-start.8 = ((bf16[128,144,128]{2,1,0:T(8,128)(2,1)}), bf16[128,144,128]{2,1,0:T(8,128)(2,1)}, u32[]{:S(2)}, u32[]{:S(2)}) async-start(bf16[128,144,128]{2,1,0:T(8,128)(2,1)} %get-tuple-element.86), calls=%async_computation.8 | async-start | bytes 9437184 | tf_op jit(solution)/shard_map/cond/branch_1_fun/all_to_all | solution.py:313
  288.9 123.4 %all-to-all-start.9 = ((bf16[128,272,128]{2,1,0:T(8,128)(2,1)}), bf16[128,272,128]{2,1,0:T(8,128)(2,1)}, u32[]{:S(2)}, u32[]{:S(2)}) async-start(bf16[128,272,128]{2,1,0:T(8,128)(2,1)} %branch_1_fun.13), calls=%async_computation.9 | async-start | bytes 17825792 | tf_op jit(solution)/shard_map/cond/branch_1_fun/all_to_all | solution.py:313
